TPU v7x, 128 devices: a whole 4x4x4 slice. The times are simulated.
128 devices in a mesh: section: 2 (over y_hi), wide: 16 (over x, y_lo, core), narrow: 4 (over z).
Axes of the slice: x: 4, y: 4 (y_hi: 2, y_lo: 2; y = y_hi * 2 + y_lo), z: 4, core: 2. Of those that a mesh axis runs over, the one named last changes fastest.
Arguments:
- boundary_grad: bfloat16 [2, 8192, 4096], P('section', 'wide', 'narrow'), may hold values from -6 to 6
- tile_target: int32 [2, 8192], P('section', 'wide'), may hold values from 0 to 15, as said below
- tile_row: int32 [2, 8192], P('section', 'wide'), may hold values from 0 to 511, as said below
- normed_input: bfloat16 [2, 8192, 4096], P('section', 'wide'), may hold values from -6 to 6
- query: bfloat16 [2, 8192, 4096], P('section', 'wide', 'narrow'), may hold values from -16 to 16
- keys: bfloat16 [2, 8192, 4096], P('section', 'wide', 'narrow'), may hold values from -5 to 5
- values: bfloat16 [2, 8192, 4096], P('section', 'wide', 'narrow'), may hold values from -6 to 6
- positions: int32 [2, 8192], P('section', 'wide'), may hold values from 0 to 511, as said below
- out_weight: bfloat16 [2, 4096, 4096], P('section', 'wide', 'narrow'), may hold values from -0.09375 to 0.09375
- value_weight: bfloat16 [2, 4096, 4096], P('section', 'wide', 'narrow'), may hold values from -0.09375 to 0.09375
Outputs:
- grad_input: bfloat16 [2, 8192, 4096], P('section', 'wide')
- grad_query: bfloat16 [2, 8192, 4096], P('section', 'wide', 'narrow')
- grad_key: bfloat16 [2, 8192, 4096], P('section', 'wide', 'narrow')
- grad_out_weight: float32 [2, 4096, 4096], P('section', 'wide', 'narrow')
- grad_value_weight: float32 [2, 4096, 4096], P('section', 'wide', 'narrow')
Inputs may be any that keep to these rules, and one draw needn't show every extreme that they name: `tile_target`: each device's 512 rows of a section go to receiving data indices; one device gives at most 48 rows to one index, exactly 48 to some, and every receiving index gets exactly 512 rows from the section. `tile_row`: together with tile_target, names every row of the receiving section exactly once. `positions`: counts the earlier tokens of the same document; documents lie inside aligned blocks of 512 rows, each block's first row has position 0, and each section's first block is one whole document.
All inputs are finite; a program needn't handle non-finite values.
Results may differ from a plain program's by a relative error of at most 0.022.
Values may be sent and summed in bfloat16 or wider, within the bound.
A program may use at most 128 MiB of HBM per device.

v0:
```python
import jax
import jax.numpy as jnp
from jax import lax
from jax.sharding import PartitionSpec as P

HEAD_DIM = 128


def partner(x, axis, stride):
    return lax.ppermute(x, axis, [(i, i ^ 1 << stride) for i in range(lax.axis_size(axis))])


def deliver(tile, targets, row_list, groups, slots):
    tok_rows = tile.shape[0]
    member = (targets[:, None] == jnp.arange(groups, dtype=jnp.int32)[None, :]).astype(jnp.int32)
    earlier = jnp.cumsum(member, axis=0) - member
    within = jnp.sum(earlier * member, axis=1)
    slot_index = targets * slots + within
    packed = jnp.zeros((groups * slots, tile.shape[1]), tile.dtype).at[slot_index].set(tile)
    places = jnp.full((groups * slots,), tok_rows, jnp.int32).at[slot_index].set(row_list)
    packed, places = partner((packed, places), "section", 0)
    packed, places = (
        lax.all_to_all(packed, "wide", split_axis=0, concat_axis=0, tiled=True),
        lax.all_to_all(places, "wide", split_axis=0, concat_axis=0, tiled=True),
    )
    canvas = jnp.zeros((tok_rows, tile.shape[1]), tile.dtype)
    return canvas.at[places].set(packed, mode="drop")


def attention_backward(query_rows, key_rows, value_rows, position_rows, grad_attended):
    tok_rows = query_rows.shape[0]
    heads_here = query_rows.shape[1] // HEAD_DIM
    scale = HEAD_DIM ** (-0.5)
    query_heads = query_rows.reshape(tok_rows, heads_here, HEAD_DIM)
    key_heads = key_rows.reshape(tok_rows, heads_here, HEAD_DIM)
    value_heads = value_rows.reshape(tok_rows, heads_here, HEAD_DIM)
    gout_heads = grad_attended.reshape(tok_rows, heads_here, HEAD_DIM)
    block_rows = min(tok_rows, 512)
    key_index = jnp.arange(tok_rows, dtype=jnp.int32)

    def one_block(carry, first_row):
        query_index = first_row + jnp.arange(block_rows, dtype=jnp.int32)
        allowed = (key_index[None, :] <= query_index[:, None]) & (
            key_index[None, :] >= (query_index - position_rows)[:, None]
        )
        scores = (
            jnp.einsum("qhe,khe->hqk", query_heads, key_heads, preferred_element_type=jnp.float32)
            * scale
        )
        scores = jnp.where(allowed[None], scores, -1e30)
        highest = jnp.max(scores, axis=-1, keepdims=True)
        weights = jnp.exp(scores - highest)
        probs = weights / jnp.sum(weights, axis=-1, keepdims=True)
        probs_low = probs.astype(jnp.bfloat16)
        attended = jnp.einsum(
            "hqk,khe->qhe", probs_low, value_heads, preferred_element_type=jnp.float32
        ).astype(jnp.bfloat16)
        dprob = jnp.einsum(
            "qhe,khe->hqk", gout_heads, value_heads, preferred_element_type=jnp.float32
        )
        delta = jnp.sum(probs * dprob, axis=-1, keepdims=True)
        dscore = (probs * (dprob - delta)).astype(jnp.bfloat16)
        value_part = jnp.einsum(
            "hqk,qhe->khe", probs_low, gout_heads, preferred_element_type=jnp.float32
        )
        key_part = jnp.einsum(
            "hqk,qhe->khe", dscore, query_heads, preferred_element_type=jnp.float32
        )
        query_grad = (
            jnp.einsum("hqk,khe->qhe", dscore, key_heads, preferred_element_type=jnp.float32)
            * scale
        ).astype(jnp.bfloat16)
        return ((carry[0] + value_part, carry[1] + key_part), (attended, query_grad))

    zeros = jnp.zeros((tok_rows, heads_here, HEAD_DIM), jnp.float32)
    block_starts = jnp.arange(tok_rows // block_rows, dtype=jnp.int32) * block_rows
    sums, stacked = lax.scan(one_block, (zeros, zeros), block_starts)
    flat_shape = (tok_rows, heads_here * HEAD_DIM)
    attended = stacked[0].reshape(flat_shape)
    grad_query = stacked[1].reshape(flat_shape)
    grad_value = sums[0].astype(jnp.bfloat16).reshape(flat_shape)
    grad_key = (sums[1] * scale).astype(jnp.bfloat16).reshape(flat_shape)
    return (attended, grad_value, grad_query, grad_key)


def shards(
    boundary_grad,
    tile_target,
    tile_row,
    normed_input,
    query,
    keys,
    values,
    positions,
    out_weight,
    value_weight,
):
    tile = boundary_grad[0]
    targets = tile_target[0]
    row_list = tile_row[0]
    tok_rows = tile.shape[0]
    groups = lax.axis_size("wide")
    slots = 3 * tok_rows // (2 * groups)
    whole_tile = lax.all_gather(tile, "narrow", axis=1, tiled=True)
    full_grad = deliver(whole_tile, targets, row_list, groups, slots)
    out_shard = out_weight[0]
    grad_cols = full_grad
    grad_attended = jnp.dot(
        grad_cols,
        lax.all_gather(out_shard, "wide", axis=0, tiled=True),
        preferred_element_type=jnp.float32,
    ).astype(jnp.bfloat16)
    attended, grad_value, grad_query, grad_key = attention_backward(
        query[0], keys[0], values[0], positions[0], grad_attended
    )
    normed = normed_input[0]
    grad_cols = full_grad
    grad_out_weight = lax.psum_scatter(
        jnp.einsum("td,th->dh", grad_cols, attended, preferred_element_type=jnp.float32).astype(
            jnp.bfloat16
        ),
        "wide",
        scatter_dimension=0,
        tiled=True,
    ).astype(jnp.float32)
    partial_input = jnp.einsum(
        "th,dh->td",
        grad_value,
        lax.all_gather(value_weight[0], "wide", axis=0, tiled=True),
        preferred_element_type=jnp.float32,
    )
    summed = lax.psum(partial_input.astype(jnp.bfloat16), "narrow").astype(jnp.float32)
    grad_input = (full_grad.astype(jnp.float32) + summed).astype(jnp.bfloat16)
    grad_value_weight = lax.psum_scatter(
        jnp.einsum("td,th->dh", normed, grad_value, preferred_element_type=jnp.float32).astype(
            jnp.bfloat16
        ),
        "wide",
        scatter_dimension=0,
        tiled=True,
    ).astype(jnp.float32)
    return (
        grad_input[None],
        grad_query[None],
        grad_key[None],
        grad_out_weight[None],
        grad_value_weight[None],
    )


def solution(mesh):
    in_specs = (
        P("section", "wide", "narrow"),
        P("section", "wide"),
        P("section", "wide"),
        P("section", "wide", None),
        P("section", "wide", "narrow"),
        P("section", "wide", "narrow"),
        P("section", "wide", "narrow"),
        P("section", "wide"),
        P("section", "wide", "narrow"),
        P("section", "wide", "narrow"),
    )
    out_specs = (
        P("section", "wide", None),
        P("section", "wide", "narrow"),
        P("section", "wide", "narrow"),
        P("section", "wide", "narrow"),
        P("section", "wide", "narrow"),
    )
    return jax.shard_map(shards, mesh=mesh, in_specs=in_specs, out_specs=out_specs, check_vma=False)
```

profile of v0, /device:TPU:27, one launch (start us, length us, event | category | flops | bytes accessed | tf_op | source)
XLA Modules:
  0.0 735.2 jit_solution(10892027861416963223)
XLA Ops:
  7.2 0.0 all-gather.7.cloned.1.call-start
  7.2 0.7 all-gather.7.cloned.1.call-update
  7.9 0.0 all-gather.9.cloned.1.call-start
  7.9 0.7 all-gather.9.cloned.1.call-update
  8.6 0.0 all-gather.11.cloned.1.call-start
  8.7 0.7 all-gather.11.cloned.1.call-update
  9.4 0.7 fusion.46
  10.1 1.1 reduce-window.6
  11.2 0.2 slice_reduce_fusion
  11.5 0.8 fusion.45
  12.2 0.7 compare_select_fusion.1
  12.9 47.4 %all-gather.7.cloned.1.call-done = bf16[1,512,4096]{2,1,0:T(8,128)(2,1)} async-done(((bf16[1,512,1024]{2,1,0:T(8,128)(2,1)}), bf16[1,512,4096]{2,1,0:T(8,128)(2,1)}) %all-gather.7.cloned.1.call-update) | async-done | bytes 4194320 | tf_op jit(solution)/shard_map/all_gather | solution.py:104
  60.3 11.5 %scatter_custom_fusion.1 = bf16[768,4096]{1,0:T(8,128)(2,1)} fusion(s32[512]{0:T(512)S(1)} %bitcast.112, bf16[1,512,4096]{2,1,0:T(8,128)(2,1)} %all-gather.7.cloned.1.call-done, bf16[]{:T(256)} %constant.14.clone.1), kind=kCustom, calls=%fused_computation.19 | custom fusion | bytes 10485762 | tf_op jit(solution)/shard_map/scatter | solution.py:19
  71.7 1.1 collective-permute-start.1
  72.9 2.6 scatter_custom_fusion
  75.5 1.9 collective-permute-start
  77.4 132.6 %collective-permute-done = s32[768]{0:T(1024)S(1)} collective-permute-done((s32[768]{0:T(1024)S(1)}, s32[768]{0:T(1024)S(1)}, u32[]{:S(2)}, u32[]{:S(2)}) %collective-permute-start) | collective-permute-done | bytes 3104 | tf_op jit(solution)/shard_map/ppermute | solution.py:10
  210.0 0.1 all_to_all.16
  210.1 85.9 %all_to_all.24 = s32[16,48,1]{1,2,0:T(1,128)S(1)} all-to-all(s32[16,48,1]{1,2,0:T(1,128)S(1)} %bitcast.108), channel_id=1, replica_groups=mesh['section'=2,'wide'=16,'narrow'=4] {'wide'}, dimensions={0} | all-to-all | bytes 6144 | tf_op jit(solution)/shard_map/all_to_all | solution.py:24
  296.0 0.0 collective-permute-done.1
  296.0 7.2 all-to-all-start.1
  303.2 0.5 all-reduce.2.cloned.1.call-start
  303.7 0.5 copy.67
  304.3 0.5 copy.68
  304.9 0.1 fusion.38
  305.0 5.4 fusion.52
  310.4 0.5 broadcast.123
  310.9 0.7 reduce.7
  311.6 0.1 all_to_all.18
  311.7 66.2 %all-to-all-done.1 = bf16[16,48,4096]{2,1,0:T(8,128)(2,1)} async-done(((bf16[16,48,4096]{2,1,0:T(8,128)(2,1)}), bf16[16,48,4096]{2,1,0:T(8,128)(2,1)}, u32[]{:S(2)}, u32[]{:S(2)}) %all-to-all-start.1) | async-done | bytes 6291488 | tf_op jit(solution)/shard_map/all_to_all | solution.py:23
  378.0 15.8 %scatter_custom_fusion.2 = bf16[512,4096]{1,0:T(8,128)(2,1)} fusion(s32[768]{0:T(1024)S(1)} %fusion.47, bf16[768,4096]{1,0:T(8,128)(2,1)} %bitcast.10, bf16[]{:T(256)} %constant.14.clone.1), kind=kCustom, calls=%fused_computation.32 | custom fusion | bytes 4194816 | tf_op jit(solution)/shard_map/scatter | solution.py:27
  393.7 0.0 all-gather.9.cloned.1.call-done
  393.8 9.3 %fusion.32 = bf16[64,8,8,128]{3,2,1,0:T(8,128)(2,1)S(1)} fusion(bf16[512,4096]{1,0:T(8,128)(2,1)} %scatter_custom_fusion.2, bf16[1,4096,1024]{2,1,0:T(8,128)(2,1)} %all-gather.9.cloned.1.call-done), kind=kOutput, calls=%fused_computation.37 | convolution fusion | flops 4295491584 | bytes 13631488 | tf_op jit(solution)/shard_map/dot_general | solution.py:108
  403.1 0.0 copy-start.8
  403.1 1.0 copy-done.8
  404.0 1.5 fusion.23
  405.6 0.0 all-gather.11.cloned.1.call-done
  405.6 9.6 %fusion.6 = bf16[512,4096]{1,0:T(8,128)(2,1)} fusion(bf16[512,1024]{0,1:T(8,128)(2,1)S(1)} %bitcast.116, bf16[1,4096,1024]{2,1,0:T(8,128)(2,1)} %all-gather.11.cloned.1.call-done), kind=kOutput, calls=%fused_computation.16 | convolution fusion | flops 4297064448 | bytes 13631488 | tf_op jit(solution)/shard_map/th,dh->td/dot_general | solution.py:126
  415.2 0.0 all-reduce.2.cloned.1.call-update
  415.3 0.0 reduce-scatter.5.cloned.1.call-start
  415.3 8.9 %convert_bitcast_fusion = bf16[4096,1024]{0,1:T(8,128)(2,1)} fusion(bf16[512,1024]{0,1:T(8,128)(2,1)S(1)} %bitcast.117, bf16[1,512,4096]{2,1,0:T(8,128)(2,1)} %param.13), kind=kOutput, calls=%fused_computation.8 | convolution fusion | flops 4299161600 | bytes 13631488 | tf_op jit(solution)/shard_map/td,th->dh/dot_general | solution.py:135
  424.2 0.0 reduce-scatter.5.cloned.1.call-update
  424.2 0.3 reduce-scatter.3.cloned.1.call-start
  424.5 0.9 copy-done.5
  425.4 1.3 copy.69
  426.7 4.6 fusion.26
  431.3 0.3 copy-done
  431.6 7.0 convolution_convert_fusion
  438.7 0.0 reduce-scatter.3.cloned.1.call-update
  438.7 1.2 copy-done.6
  439.9 5.1 multiply_reduce_fusion
  445.0 4.6 multiply_convert_fusion
  449.6 2.0 copy-done.1
  451.5 1.5 multiply_convert_fusion.1
  453.0 1.3 copy.61
  454.4 2.9 multiply_convert_fusion.2
  457.3 1.3 copy.60
  458.6 70.6 %all-reduce.2.cloned.1.call-done = bf16[512,4096]{1,0:T(8,128)(2,1)} async-done(((bf16[512,4096]{1,0:T(8,128)(2,1)}), bf16[512,4096]{1,0:T(8,128)(2,1)}) %all-reduce.2.cloned.1.call-update) | async-done | bytes 4194320 | tf_op jit(solution)/shard_map/psum | solution.py:132
  529.2 7.2 fusion.9
  536.5 89.6 %reduce-scatter.5.cloned.1.call-done = bf16[256,1024]{0,1:T(8,128)(2,1)} async-done(((bf16[4096,1024]{0,1:T(8,128)(2,1)}), bf16[256,1024]{0,1:T(8,128)(2,1)}) %reduce-scatter.5.cloned.1.call-update) | async-done | bytes 524304 | tf_op jit(solution)/shard_map/reduce_scatter | solution.py:134
  626.1 1.1 bitcast_convert_fusion
  627.2 1.3 copy.62
  628.5 97.5 %reduce-scatter.3.cloned.1.call-done = bf16[256,1024]{1,0:T(8,128)(2,1)} async-done(((bf16[4096,1024]{1,0:T(8,128)(2,1)}), bf16[256,1024]{1,0:T(8,128)(2,1)}) %reduce-scatter.3.cloned.1.call-update) | async-done | bytes 524304 | tf_op jit(solution)/shard_map/reduce_scatter | solution.py:118
  726.0 2.1 bitcast_convert_fusion.1
  (16 shorter events, 0.1 us)
Async XLA Ops:
  7.2 53.1 %all-gather.7.cloned.1.call-start = ((), (), s32[]{:S(2)}) async-start(), calls=%async_computation.7 | async-start | bytes 5242880 | tf_op jit(solution)/shard_map/all_gather | solution.py:104
  7.9 385.9 %all-gather.9.cloned.1.call-start = ((), (), s32[]{:S(2)}) async-start(), calls=%async_computation.8 | async-start | bytes 8912896 | tf_op jit(solution)/shard_map/all_gather | solution.py:110
  8.6 396.9 %all-gather.11.cloned.1.call-start = ((), (), s32[]{:S(2)}) async-start(), calls=%async_computation.9 | async-start | bytes 8912896 | tf_op jit(solution)/shard_map/all_gather | solution.py:129
  71.7 224.2 %collective-permute-start.1 = (bf16[768,4096]{1,0:T(8,128)(2,1)}, bf16[768,4096]{1,0:T(8,128)(2,1)}, u32[]{:S(2)}, u32[]{:S(2)}) collective-permute-start(bf16[768,4096]{1,0:T(8,128)(2,1)} %scatter_custom_fusion.1), channel_id=1, source_target_pairs={{0,64},{64,0},{1,65},{65,1},{2,66},{66,2},{3,67},{67,3},{4,68},{68... | collective-permute-start | bytes 18874376 | tf_op jit(solution)/shard_map/ppermute | solution.py:10
  75.5 134.5 %collective-permute-start = (s32[768]{0:T(1024)S(1)}, s32[768]{0:T(1024)S(1)}, u32[]{:S(2)}, u32[]{:S(2)}) collective-permute-start(s32[768]{0:T(1024)S(1)} %scatter_custom_fusion), channel_id=1, source_target_pairs={{0,64},{64,0},{1,65},{65,1},{2,66},{66,2},{3,67},{67,3},{4,68},{68... | collective-permute-start | bytes 9224 | tf_op jit(solution)/shard_map/ppermute | solution.py:10
  296.0 7.8 %copy-start.3 = (bf16[1,512,1024]{2,1,0:T(8,128)(2,1)S(1)}, bf16[1,512,1024]{2,1,0:T(8,128)(2,1)}, u32[]{:S(2)}) copy-start(bf16[1,512,1024]{2,1,0:T(8,128)(2,1)} %param.14) | copy-start | bytes 3145732
  296.0 8.3 %copy-start.4 = (bf16[1,512,1024]{2,1,0:T(8,128)(2,1)S(1)}, bf16[1,512,1024]{2,1,0:T(8,128)(2,1)}, u32[]{:S(2)}) copy-start(bf16[1,512,1024]{2,1,0:T(8,128)(2,1)} %param.15) | copy-start | bytes 3145732
  296.0 8.9 %copy-start.7 = (s32[1,512]{1,0:T(1,128)S(1)}, s32[1,512]{1,0:T(1,128)}, u32[]{:S(2)}) copy-start(s32[1,512]{1,0:T(1,128)} %param.17) | copy-start | bytes 6148
  296.0 82.0 %all-to-all-start.1 = ((bf16[16,48,4096]{2,1,0:T(8,128)(2,1)}), bf16[16,48,4096]{2,1,0:T(8,128)(2,1)}, u32[]{:S(2)}, u32[]{:S(2)}) async-start(bf16[16,48,4096]{2,1,0:T(8,128)(2,1)} %bitcast.9), calls=%async_computation.1 | async-start | bytes 12582912 | tf_op jit(solution)/shard_map/all_to_all | solution.py:23
  303.2 226.0 %all-reduce.2.cloned.1.call-start = ((), (), s32[]{:S(2)}) async-start(), calls=%async_computation.4 | async-start | bytes 8388608 | tf_op jit(solution)/shard_map/psum | solution.py:132
  393.8 10.3 %copy-start.2 = (f32[8,512,512]{1,2,0:T(8,128)S(1)}, f32[8,512,512]{1,2,0:T(8,128)}, u32[]{:S(2)}) copy-start(f32[8,512,512]{1,2,0:T(8,128)} %get-tuple-element.54) | copy-start | bytes 25165828
  403.1 1.0 copy-start.8
  415.3 210.8 %reduce-scatter.5.cloned.1.call-start = ((), (), s32[]{:S(2)}) async-start(), calls=%async_computation.6 | async-start | bytes 8912896 | tf_op jit(solution)/shard_map/reduce_scatter | solution.py:134
  424.2 1.2 copy-start.5
  424.2 301.8 %reduce-scatter.3.cloned.1.call-start = ((), (), s32[]{:S(2)}) async-start(), calls=%async_computation.5 | async-start | bytes 8912896 | tf_op jit(solution)/shard_map/reduce_scatter | solution.py:118
  426.7 4.9 copy-start
  438.7 1.2 copy-start.6
  449.6 2.0 copy-start.1
Sparse Core Ops, SparseCore 0:
  9.7 50.5 all-gather.6
  62.0 82.4 all-gather.8
  146.2 92.6 all-gather.10
  415.4 113.7 all-reduce.1
  531.6 94.4 reduce-scatter.4
  628.5 97.5 reduce-scatter.2
where the time goes:
time: 747 us; the launch traced here: 735 us
  waiting for transfers between devices  506 us (68%)
  blocking collectives  85.9 us (11%)
  matrix products  55.8 us (7%)
  local copies, waits for them, and re-layouts  42.4 us (6%)
  other arithmetic  19.2 us (3%)
  between operations  14.5 us (2%)
  starting transfers between devices  11.2 us (1%)
    ppermute x2, waiting for transfers between devices, partner(): lax.ppermute(x, axis, [(i, i ^ 1 << stride) for i in range(lax.axis_size(...  133 us
    reduce_scatter x1, waiting for transfers between devices, shards(): lax.psum_scatter(jnp.einsum('td,th->dh', grad_cols, attended, preferred_e...  97.5 us
    reduce_scatter x1, waiting for transfers between devices, shards(): lax.psum_scatter(jnp.einsum('td,th->dh', normed, grad_value, preferred_el...  89.6 us
    all_to_all x1, blocking collectives, deliver(): lax.all_to_all(places, 'wide', split_axis=0, concat_axis=0, tiled=True)  85.9 us
    psum x1, waiting for transfers between devices, shards(): lax.psum(partial_input.astype(jnp.bfloat16), 'narrow').astype(jnp.float32)  70.6 us
    all_to_all x1, waiting for transfers between devices, deliver(): lax.all_to_all(packed, 'wide', split_axis=0, concat_axis=0, tiled=True)  66.2 us
    all_gather x1, waiting for transfers between devices, shards(): whole_tile = lax.all_gather(tile, 'narrow', axis=1, tiled=True)  47.4 us
    scatter x1, local copies, waits for them, and re-layouts, deliver(): return canvas.at[places].set(packed, mode='drop')  15.8 us
  transfers between devices with their start and end apart: 9, of which 6 were waited for; matrix products, arithmetic and copies ran while one was open for 14% of the time, Pallas kernels for 0%

commit v1 on v0

v1 whole, which is shorter than its diff:
```python
import functools

import jax
import jax.numpy as jnp
from jax import lax
from jax.experimental import pallas as pl
from jax.experimental.pallas import tpu as pltpu
from jax.sharding import PartitionSpec as P

HEAD_DIM = 128
MESH = pl.DeviceIdType.MESH
SLOTS = 48
PAD = 64


class Place:
    def __init__(self):
        self.s = lax.axis_index("section")
        self.w = lax.axis_index("wide")
        self.n = lax.axis_index("narrow")
        self.core = self.w % 2
        self.y = (self.w // 2) % 2
        self.x = self.w // 4
        self.w_xp = (self.w + 4) % 16
        self.w_xm = (self.w + 12) % 16
        self.w_x2 = (self.w + 8) % 16
        self.w_y = self.w + 2 - 4 * self.y
        self.w_core = self.w + 1 - 2 * self.core
        self.y_xp = (self.w_y + 4) % 16
        self.y_xm = (self.w_y + 12) % 16
        self.y_x2 = (self.w_y + 8) % 16
        self.n_p = (self.n + 1) % 4
        self.n_m = (self.n + 3) % 4
        self.n_2 = (self.n + 2) % 4

    def wide(self, w):
        return (self.s, w, self.n)

    def narrow(self, n):
        return (self.s, self.w, n)


class Links:
    def __init__(self, send_sem, recv_sem):
        self.send_sem, self.recv_sem, self.count, self.sent = send_sem, recv_sem, 0, []

    def put(self, src, dst, device):
        copy = pltpu.make_async_remote_copy(
            src_ref=src,
            dst_ref=dst,
            send_sem=self.send_sem.at[self.count],
            recv_sem=self.recv_sem.at[self.count],
            device_id=device,
            device_id_type=MESH,
        )
        copy.start()
        self.count += 1
        self.sent.append(copy)
        return copy

    def drain(self):
        for copy in self.sent:
            copy.wait_send()


def greet(devices):
    barrier = pltpu.get_barrier_semaphore()
    for device in devices:
        pl.semaphore_signal(barrier, inc=1, device_id=device, device_id_type=MESH)
    return barrier


def gather_wide(at, links, own, full, local_sem):
    half = own.shape[0] // 2
    lower, upper = pl.ds(0, half), pl.ds(half, half)
    third, fourth = pl.ds(half, half // 2), pl.ds(half + half // 2, half // 2)
    xp, xm, yy, cc = (at.wide(w) for w in (at.w_xp, at.w_xm, at.w_y, at.w_core))

    def send(w, device, rows=None):
        ref = full.at[w] if rows is None else full.at[w, rows]
        return links.put(ref, ref, device)

    state = {}

    def first():
        state["own"] = pltpu.make_async_copy(own, full.at[at.w], local_sem)
        state["own"].start()
        state["y"] = links.put(own, full.at[at.w], yy)
        state["xp"] = links.put(own, full.at[at.w], xp)
        state["xm"] = links.put(own, full.at[at.w], xm)
        state["core"] = links.put(own, full.at[at.w], cc)

    def second_y():
        state["y"].wait_recv()
        state["b_p"] = send(at.w_y, xp, upper)
        state["b_m"] = send(at.w_y, xm, upper)
        state["c_y"] = send(at.w_y, cc)

    def second_x():
        state["xp"].wait_recv()
        state["f_p"] = send(at.w_xm, xp, lower)
        state["g_m"] = send(at.w_xm, yy, lower)
        state["c_m"] = send(at.w_xm, cc)
        state["xm"].wait_recv()
        state["f_m"] = send(at.w_xp, xm, upper)
        state["g_p"] = send(at.w_xp, yy, lower)
        state["c_p"] = send(at.w_xp, cc)

    def third_step():
        state["b_p"].wait_recv()
        state["h_p"] = send(at.y_xm, xp, third)
        state["b_m"].wait_recv()
        state["h_m"] = send(at.y_xp, xm, fourth)
        state["f_p"].wait_recv()
        state["g_2"] = send(at.w_x2, yy, lower)
        state["f_m"].wait_recv()
        state["c_2"] = send(at.w_x2, cc)

    def fourth_step():
        state["g_m"].wait_recv()
        state["e_m"] = send(at.y_xm, cc)
        state["g_p"].wait_recv()
        state["e_p"] = send(at.y_xp, cc)
        state["h_p"].wait_recv()
        state["h_m"].wait_recv()
        state["g_2"].wait_recv()
        state["e_2"] = send(at.y_x2, cc)

    def last():
        state["own"].wait()
        for name in ("core", "c_y", "c_m", "c_p", "c_2", "e_m", "e_p", "e_2"):
            state[name].wait_recv()

    return first, second_y, second_x, third_step, fourth_step, last


def relay_kernel(
    tile_ref, target_ref, row_ref, wo_ref, vw_ref,
    g_ref, wo_all, vw_all,
    packed, places, landed, landed_places, spread, canvas, vw_own,
    send_sem, recv_sem, data_send, data_recv, place_send, place_recv, share_send, share_recv, local_sem,
):
    at = Place()
    groups = 16
    tok = tile_ref.shape[0]
    barrier = greet(
        [(1 - at.s, t, at.n) for t in range(groups)]
        + [at.wide(w) for w in (at.w_xp, at.w_xm, at.w_y)]
        + [(at.s, w, n) for w in (at.w, at.w_core) for n in (at.n_p, at.n_m, at.n_2)]
        + [at.wide(at.w_core)]
    )

    target = target_ref[...]
    group = lax.broadcasted_iota(jnp.int32, (groups, tok), 0)
    member = jnp.where(group == target, 1.0, 0.0).astype(jnp.float32)
    before = jnp.where(
        lax.broadcasted_iota(jnp.int32, (tok, tok), 0) < lax.broadcasted_iota(jnp.int32, (tok, tok), 1), 1.0, 0.0
    ).astype(jnp.bfloat16)
    earlier = jnp.dot(member.astype(jnp.bfloat16), before, preferred_element_type=jnp.float32)
    within = jnp.sum(earlier * member, axis=0, keepdims=True).astype(jnp.int32)
    slot = target * SLOTS + within
    choose = jnp.where(
        lax.broadcasted_iota(jnp.int32, (groups * SLOTS, tok), 0) == slot, 1.0, 0.0
    ).astype(jnp.bfloat16)
    packed[...] = jnp.dot(choose, tile_ref[...], preferred_element_type=jnp.float32).astype(jnp.bfloat16)

    lane = within + PAD * (at.w % 2)
    to_lane = jnp.where(
        lax.broadcasted_iota(jnp.int32, (128, tok), 0) == lane, 1.0, 0.0
    ).astype(jnp.bfloat16)
    place = row_ref[...] + 1
    high = (place // 32).astype(jnp.float32)
    low = (place % 32).astype(jnp.float32)
    nt = (((1,), (1,)), ((), ()))
    high = lax.dot_general((member * high).astype(jnp.bfloat16), to_lane, nt, preferred_element_type=jnp.float32)
    low = lax.dot_general((member * low).astype(jnp.bfloat16), to_lane, nt, preferred_element_type=jnp.float32)
    lanes = (high * 32.0 + low).astype(jnp.int32)
    places[...] = jnp.broadcast_to(lanes[:, None, :], places.shape)
    landed[:, SLOTS:, :] = jnp.zeros((groups, PAD - SLOTS, landed.shape[2]), landed.dtype)

    pl.semaphore_wait(barrier, groups + 3 + 6 + 1)

    def relay(i):
        t = (at.w + i) % groups
        device = (1 - at.s, t, at.n)
        data = pltpu.make_async_remote_copy(
            src_ref=packed.at[pl.ds(pl.multiple_of(t * SLOTS, 16), SLOTS)],
            dst_ref=landed.at[at.w, pl.ds(0, SLOTS)],
            send_sem=data_send.at[t],
            recv_sem=data_recv.at[at.w],
            device_id=device,
            device_id_type=MESH,
        )
        where = pltpu.make_async_remote_copy(
            src_ref=places.at[t],
            dst_ref=landed_places.at[at.w],
            send_sem=place_send.at[t],
            recv_sem=place_recv.at[at.w],
            device_id=device,
            device_id_type=MESH,
        )
        return data, where

    @pl.loop(0, groups)
    def _(i):
        data, where = relay(i)
        where.start()
        data.start()

    links = Links(send_sem, recv_sem)
    half_chunk = vw_ref.shape[0] // 4

    def share(h, c):
        w, n = at.w - at.core + c, 2 * at.core + h
        src = vw_ref.at[pl.ds((2 * h + c) * half_chunk, half_chunk)]
        dst = vw_own.at[pl.ds(pl.multiple_of(at.n * half_chunk, half_chunk), half_chunk)]
        mine = (at.core == c) & (at.n == n)
        remote = pltpu.make_async_remote_copy(
            src_ref=src, dst_ref=dst, send_sem=share_send.at[2 * h + c], recv_sem=share_recv.at[at.n],
            device_id=(at.s, w, n), device_id_type=MESH,
        )
        local = pltpu.make_async_copy(src, dst, share_recv.at[at.n])
        return mine, remote, local

    for h in range(2):
        for c in range(2):
            mine, remote, local = share(h, c)

            @pl.when(mine)
            def _():
                local.start()

            @pl.when(jnp.logical_not(mine))
            def _():
                remote.start()

    out_steps = gather_wide(at, links, wo_ref, wo_all, local_sem.at[0])
    value_steps = gather_wide(at, links, vw_own, vw_all, local_sem.at[1])
    out_steps[0]()

    for b in range(4):
        piece = vw_own.at[pl.ds(b * half_chunk, half_chunk)]
        pltpu.make_async_copy(piece, piece, share_recv.at[b]).wait()
    value_steps[0]()
    out_steps[1]()
    out_steps[2]()

    @pl.loop(0, groups)
    def _(i):
        data_piece = landed.at[i, pl.ds(0, SLOTS)]
        pltpu.make_async_copy(data_piece, data_piece, data_recv.at[i]).wait()
        place_piece = landed_places.at[i]
        pltpu.make_async_copy(place_piece, place_piece, place_recv.at[i]).wait()

    arrived = landed_places[...].reshape(groups // 2, 2, 8, 128)
    arrived = (arrived[:, 0] + arrived[:, 1])[:, 0, :]
    token = lax.broadcasted_iota(jnp.int32, (tok, 128), 0) + 1
    for k in range(groups // 2):
        spread[:, k * 128 : (k + 1) * 128] = jnp.where(token == arrived[k : k + 1, :], 1.0, 0.0).astype(jnp.bfloat16)
    rows = landed[...].reshape(groups * PAD, landed.shape[2])
    part = tok // 2
    z_p, z_m, z_local = [], [], []
    for h in range(2):
        span = pl.ds(h * part, part)
        canvas[span, :] = jnp.dot(spread[span, :], rows, preferred_element_type=jnp.float32).astype(jnp.bfloat16)
        z_p.append(links.put(canvas.at[span], g_ref.at[at.n, span], at.narrow(at.n_p)))
        z_m.append(links.put(canvas.at[span], g_ref.at[at.n, span], at.narrow(at.n_m)))
    z_own = pltpu.make_async_copy(canvas, g_ref.at[at.n], local_sem.at[2])
    z_own.start()

    out_steps[3]()
    value_steps[1]()
    value_steps[2]()
    out_steps[4]()

    first, second = pl.ds(0, part), pl.ds(part, part)
    z_p[0].wait_recv()
    ref = g_ref.at[at.n_m, first]
    on_p = links.put(ref, ref, at.narrow(at.n_p))
    z_m[0].wait_recv()
    z_m[1].wait_recv()
    ref = g_ref.at[at.n_p, second]
    on_m = links.put(ref, ref, at.narrow(at.n_m))
    z_p[1].wait_recv()

    value_steps[3]()
    value_steps[4]()
    on_p.wait_recv()
    on_m.wait_recv()
    z_own.wait()
    out_steps[5]()
    value_steps[5]()

    @pl.loop(0, groups)
    def _(i):
        data, where = relay(i)
        data.wait_send()
        where.wait_send()

    for h in range(2):
        for c in range(2):
            mine, remote, local = share(h, c)

            @pl.when(jnp.logical_not(mine))
            def _():
                remote.wait_send()

    links.drain()


def relay_and_gather(tile, target, row, wo, vw):
    tok, width = tile.shape
    bf16 = jnp.bfloat16
    dma = pltpu.SemaphoreType.DMA
    vmem = pl.BlockSpec(memory_space=pltpu.VMEM)
    hbm = pl.BlockSpec(memory_space=pl.ANY)
    copies = 46
    return pl.pallas_call(
        relay_kernel,
        out_shape=(
            jax.ShapeDtypeStruct((4, tok, width), bf16),
            jax.ShapeDtypeStruct((16,) + wo.shape, bf16),
            jax.ShapeDtypeStruct((16,) + vw.shape, bf16),
        ),
        in_specs=[vmem] * 5,
        out_specs=(hbm, hbm, hbm),
        scratch_shapes=[
            pltpu.VMEM((16 * SLOTS, width), bf16),
            pltpu.VMEM((16, 8, 128), jnp.int32),
            pltpu.VMEM((16, PAD, width), bf16),
            pltpu.VMEM((16, 8, 128), jnp.int32),
            pltpu.VMEM((tok, 16 * PAD), bf16),
            pltpu.VMEM((tok, width), bf16),
            pltpu.VMEM(vw.shape, bf16),
            dma((copies,)), dma((copies,)),
            dma((16,)), dma((16,)), dma((16,)), dma((16,)),
            dma((4,)), dma((4,)), dma((3,)),
        ],
        compiler_params=pltpu.CompilerParams(
            collective_id=0, has_side_effects=True, vmem_limit_bytes=40 * 1024 * 1024
        ),
        name="relay_and_gather",
    )(tile, target, row, wo, vw)


def attention_backward(query_rows, key_rows, value_rows, position_rows, grad_attended):
    tok_rows = query_rows.shape[0]
    heads_here = query_rows.shape[1] // HEAD_DIM
    scale = HEAD_DIM ** (-0.5)
    query_heads = query_rows.reshape(tok_rows, heads_here, HEAD_DIM)
    key_heads = key_rows.reshape(tok_rows, heads_here, HEAD_DIM)
    value_heads = value_rows.reshape(tok_rows, heads_here, HEAD_DIM)
    gout_heads = grad_attended.reshape(tok_rows, heads_here, HEAD_DIM)
    index = jnp.arange(tok_rows, dtype=jnp.int32)
    allowed = (index[None, :] <= index[:, None]) & (index[None, :] >= (index - position_rows)[:, None])
    f32 = dict(preferred_element_type=jnp.float32)
    scores = jnp.einsum("qhe,khe->hqk", query_heads, key_heads, **f32) * scale
    scores = jnp.where(allowed[None], scores, -1e30)
    weights = jnp.exp(scores - jnp.max(scores, axis=-1, keepdims=True))
    probs = weights / jnp.sum(weights, axis=-1, keepdims=True)
    probs_low = probs.astype(jnp.bfloat16)
    attended = jnp.einsum("hqk,khe->qhe", probs_low, value_heads, **f32).astype(jnp.bfloat16)
    dprob = jnp.einsum("qhe,khe->hqk", gout_heads, value_heads, **f32)
    delta = jnp.sum(probs * dprob, axis=-1, keepdims=True)
    dscore = (probs * (dprob - delta)).astype(jnp.bfloat16)
    grad_value = jnp.einsum("hqk,qhe->khe", probs_low, gout_heads, **f32).astype(jnp.bfloat16)
    grad_key = (jnp.einsum("hqk,qhe->khe", dscore, query_heads, **f32) * scale).astype(jnp.bfloat16)
    grad_query = (jnp.einsum("hqk,khe->qhe", dscore, key_heads, **f32) * scale).astype(jnp.bfloat16)
    flat = (tok_rows, heads_here * HEAD_DIM)
    return tuple(a.reshape(flat) for a in (attended, grad_value, grad_query, grad_key))


def shards(boundary_grad, tile_target, tile_row, normed_input, query, keys, values, positions, out_weight, value_weight):
    f32 = dict(preferred_element_type=jnp.float32)
    full_grad, out_all, value_all = relay_and_gather(
        boundary_grad[0], tile_target, tile_row, out_weight[0], value_weight[0]
    )
    tok, width = full_grad.shape[1:]
    grad_attended = jnp.einsum("btd,bdh->th", full_grad, out_all.reshape(4, width, width), **f32).astype(jnp.bfloat16)
    attended, grad_value, grad_query, grad_key = attention_backward(
        query[0], keys[0], values[0], positions[0], grad_attended
    )

    def scattered(term):
        return lax.psum_scatter(
            term.astype(jnp.bfloat16), "wide", scatter_dimension=0, tiled=True
        ).astype(jnp.float32)

    out_term = jnp.einsum("btd,th->bdh", full_grad, attended, **f32).reshape(4 * width, width)
    grad_out_weight = scattered(out_term)
    value_term = jnp.einsum("td,th->dh", normed_input[0], grad_value, **f32)
    grad_value_weight = scattered(value_term)
    gv_all = lax.all_gather(grad_value, "narrow", axis=0)
    piece = jnp.einsum("btk,jcbik->tjci", gv_all, value_all.reshape(8, 2, 4, 64, width), **f32).reshape(tok, 8, 128)
    whole = jnp.transpose(full_grad, (1, 0, 2)).reshape(tok, 8, 4, 128)
    mine = lax.dynamic_slice_in_dim(whole, lax.axis_index("narrow"), 1, 2)[:, :, 0]
    piece = (mine.astype(jnp.float32) + piece).astype(jnp.bfloat16)
    grad_input = lax.all_gather(piece, "narrow", axis=2).reshape(tok, 4 * width)
    return (grad_input[None], grad_query[None], grad_key[None], grad_out_weight[None], grad_value_weight[None])


def solution(mesh):
    split = P("section", "wide", "narrow")
    rows = P("section", "wide")
    in_specs = (split, rows, rows, P("section", "wide", None), split, split, split, rows, split, split)
    out_specs = (P("section", "wide", None), split, split, split, split)
    return jax.shard_map(shards, mesh=mesh, in_specs=in_specs, out_specs=out_specs, check_vma=False)
```

time: 747 us -> 432 us (0.58); the launches traced: 735 us -> 428 us
  waiting for transfers between devices: 506 us -> 174 us
  Pallas kernels: 0 us -> 115 us
  blocking collectives: 85.9 us -> 0 us
  local copies, waits for them, and re-layouts: 42.4 us -> 54.3 us
  starting transfers between devices: 11.2 us -> 0.57 us
  other arithmetic: 19.2 us -> 8.59 us
    ppermute x2 -> x0, waiting for transfers between devices: 133 us -> none  [partner(): lax.ppermute(x, axis, [(i, i ^ 1 << stride) for i in range(lax.axis_size(...]
    pallas_call x0 -> x1, Pallas kernels: none -> 115 us  [relay_and_gather(): pl.pallas_call(relay_kernel, out_shape=(jax.ShapeDtypeStruct((4, tok, wid...]
    all_to_all x1 -> x0, blocking collectives: 85.9 us -> none  [deliver(): lax.all_to_all(places, 'wide', split_axis=0, concat_axis=0, tiled=True)]
    psum x1 -> x0, waiting for transfers between devices: 70.6 us -> none  [shards(): lax.psum(partial_input.astype(jnp.bfloat16), 'narrow').astype(jnp.float32)]
    all_to_all x1 -> x0, waiting for transfers between devices: 66.2 us -> none  [deliver(): lax.all_to_all(packed, 'wide', split_axis=0, concat_axis=0, tiled=True)]
    reduce_scatter x2, waiting for transfers between devices: 187 us -> 137 us  [scattered(): lax.psum_scatter(term.astype(jnp.bfloat16), 'wide', scatter_dimension=0,...]
    scatter x3 -> x0, local copies, waits for them, and re-layouts: 29.8 us -> none  [the longest x1 15.8 us: deliver(): return canvas.at[places].set(packed, mode='drop')]
    dot_general x0 -> x2, local copies, waits for them, and re-layouts: none -> 14.8 us  [the longest x1 8.4 us: shards(): jnp.einsum('btk,jcbik->tjci', gv_all, value_all.reshape(8, 2, 4, 64, widt...]
  transfers between devices with their start and end apart: 9 -> 4, of which waited for: 6 -> 4; matrix products, arithmetic and copies ran while one was open for 14% -> 18% of each run, Pallas kernels for 0% -> 0%
where the time goes in v1:
time: 432 us; the launch traced here: 428 us
  waiting for transfers between devices  174 us (40%)
  Pallas kernels  115 us (27%)
  matrix products  59.6 us (14%)
  local copies, waits for them, and re-layouts  54.3 us (13%)
  between operations  15.6 us (4%)
  other arithmetic  8.59 us (2%)
    reduce_scatter x2, waiting for transfers between devices, scattered(): lax.psum_scatter(term.astype(jnp.bfloat16), 'wide', scatter_dimension=0,...  137 us
    pallas_call x1, Pallas kernels, relay_and_gather(): pl.pallas_call(relay_kernel, out_shape=(jax.ShapeDtypeStruct((4, tok, wid...  115 us
    all_gather x1, waiting for transfers between devices, shards(): gv_all = lax.all_gather(grad_value, 'narrow', axis=0)  33.7 us
    unnamed x29, local copies, waits for them, and re-layouts  19.6 us
    dot_general x1, matrix products, shards(): jnp.einsum('btd,bdh->th', full_grad, out_all.reshape(4, width, width), **...  9.52 us
    dot_general x1, matrix products, shards(): jnp.einsum('btk,jcbik->tjci', gv_all, value_all.reshape(8, 2, 4, 64, widt...  9.24 us
    dot_general x1, matrix products, shards(): value_term = jnp.einsum('td,th->dh', normed_input[0], grad_value, **f32)  8.84 us
  transfers between devices with their start and end apart: 4, of which 4 were waited for; matrix products, arithmetic and copies ran while one was open for 18% of the time, Pallas kernels for 0%

profile of v1, /device:TPU:27, one launch (start us, length us, event | category | flops | bytes accessed | tf_op | source)
XLA Modules:
  0.0 427.9 jit_solution(1659506388372542813)
XLA Ops:
  8.0 0.0 all-gather.4.cloned.1.call-start
  8.0 0.7 iota_subtract_fusion
  8.7 0.1 fusion.25
  8.9 1.5 copy.82
  10.4 1.5 copy.83
  11.9 0.0 copy-start.1
  11.9 1.2 copy-done.1
  13.1 0.0 copy-start.2
  13.1 1.0 copy-done.2
  14.2 0.0 copy-start.3
  14.2 1.0 copy-done.3
  15.2 0.0 copy-start.4
  15.2 0.7 copy-done.4
  15.9 0.7 copy-done.5
  16.6 115.3 %relay_and_gather.1 = (bf16[4,512,1024]{2,1,0:T(8,128)(2,1)S(1)}, bf16[16,256,1024]{2,1,0:T(8,128)(2,1)}, bf16[16,256,1024]{2,1,0:T(8,128)(2,1)}) custom-call(bf16[512,1024]{1,0:T(8,128)(2,1)S(1)} %bitcast.84, s32[1,512]{1,0:T(1,128)S(1)} %copy-done.4, s32[1,512]{1,0:T(1,128)S(1)} %copy-done.5, bf16[256,1024]{1,0:T(8,128)(2,1)S(1)} %bitcast.85, ...), custom_call_target="tpu_custom_call" | custom-call | tf_op jit(solution)/shard_map/relay_and_gather/pallas_call | solution.py:318
  131.9 0.0 copy-start
  131.9 9.5 %fusion.21 = bf16[64,8,8,128]{3,2,1,0:T(8,128)(2,1)} fusion(bf16[4,512,1024]{2,1,0:T(8,128)(2,1)S(1)} %get-tuple-element.8, bf16[4,1024,1024]{2,1,0:T(8,128)(2,1)} %bitcast.103), kind=kOutput, calls=%fused_computation.26 | convolution fusion | flops 4295491584 | bytes 13631488 | tf_op jit(solution)/shard_map/btd,bdh->th/dot_general | solution.py:379
  141.4 0.0 copy-done
  141.4 5.4 %fusion.32 = (f32[8,512]{1,0:T(8,128)S(1)}, f32[8,512,512]{1,2,0:T(8,128)}) fusion(pred[512,512]{0,1:T(8,128)(4,1)S(1)} %fusion.25, bf16[512,8,128]{0,2,1:T(8,128)(2,1)S(1)} %bitcast.95, bf16[512,8,128]{0,2,1:T(8,128)(2,1)S(1)} %bitcast.92), kind=kOutput, calls=%fused_computation.42 | convolution fusion | flops 545260032 | bytes 10764288 | tf_op jit(solution)/shard_map/sub | solution.py:359
  146.8 5.2 %fusion.15 = bf16[8,128,512]{2,1,0:T(8,128)(2,1)S(1)} fusion(bf16[64,8,8,128]{3,2,1,0:T(8,128)(2,1)} %fusion.21, f32[8,512,512]{1,2,0:T(8,128)} %get-tuple-element.27, f32[8,512]{1,0:T(8,128)S(1)} %get-tuple-element.26), kind=kOutput, calls=%fused_computation.24 | convolution fusion | flops 541589504 | bytes 10502144 | tf_op jit(solution)/shard_map/hqk,qhe->khe/dot_general | solution.py:366
  152.1 0.0 copy-start.9
  152.1 1.3 copy.60
  153.4 0.0 all-gather.4.cloned.1.call-update
  153.4 0.2 all-gather.6.cloned.1.call-start
  153.7 8.4 %copy.61 = bf16[8,2,64,4,1024]{4,2,1,3,0:T(8,128)(2,1)} copy(bf16[8,2,64,4,1024]{4,2,3,1,0:T(8,128)(2,1)} %bitcast.89) | data formatting | bytes 16777216 | tf_op jit(solution)/shard_map/btk,jcbik->tjci/dot_general | solution.py:394
  162.1 0.0 copy-done.9
  162.1 6.4 %copy.54 = bf16[512,4,1024]{0,2,1:T(8,128)(2,1)} copy(bf16[512,4,1024]{2,0,1:T(8,128)(2,1)} %bitcast.82) | data formatting | bytes 8388608 | tf_op jit(solution)/shard_map/transpose | solution.py:395
  168.4 1.4 constant_dynamic-slice_fusion
  169.9 1.3 copy.81
  171.2 33.7 %all-gather.4.cloned.1.call-done = bf16[4,512,1024]{2,1,0:T(8,128)(2,1)} async-done(((bf16[1,512,1024]{2,1,0:T(8,128)(2,1)}), bf16[4,512,1024]{2,1,0:T(8,128)(2,1)}) %all-gather.4.cloned.1.call-update) | async-done | bytes 4194320 | tf_op jit(solution)/shard_map/all_gather | solution.py:393
  204.8 0.0 copy-start.10
  204.8 9.2 %fusion.8 = bf16[512,8,128]{2,0,1:T(8,128)(2,1)} fusion(bf16[8,128,4,1024]{3,1,2,0:T(8,128)(2,1)} %bitcast.88, bf16[4,512,1024]{2,1,0:T(8,128)(2,1)} %all-gather.4.cloned.1.call-done, bf16[512,8,1,128]{3,0,1,2:T(8,128)(2,1)} %copy.81), kind=kOutput, calls=%fused_computation.16 | convolution fusion | flops 4296540160 | bytes 14680064 | tf_op jit(solution)/shard_map/btk,jcbik->tjci/dot_general | solution.py:394
  214.1 0.0 all-gather.6.cloned.1.call-update
  214.1 0.0 reduce-scatter.5.cloned.1.call-start
  214.1 0.0 copy-done.10
  214.2 8.8 %convert_bitcast_fusion = bf16[4096,1024]{0,1:T(8,128)(2,1)} fusion(bf16[512,1024]{0,1:T(8,128)(2,1)S(1)} %bitcast.98, bf16[1,512,4096]{2,1,0:T(8,128)(2,1)} %param.13), kind=kOutput, calls=%fused_computation.1 | convolution fusion | flops 4299161600 | bytes 13631488 | tf_op jit(solution)/shard_map/td,th->dh/dot_general | solution.py:391
  223.0 0.0 copy-start.8
  223.0 0.0 reduce-scatter.5.cloned.1.call-update
  223.0 0.3 reduce-scatter.3.cloned.1.call-start
  223.3 1.0 copy-done.8
  224.3 1.3 copy.84
  225.6 0.0 copy-start.11
  225.6 6.4 %copy.69 = bf16[4,1024,512]{2,1,0:T(8,128)(2,1)} copy(bf16[4,1024,512]{1,2,0:T(8,128)(2,1)} %bitcast.83) | data formatting | bytes 8388608 | tf_op jit(solution)/shard_map/btd,th->bdh/dot_general | solution.py:389
  232.0 0.0 copy-done.11
  232.0 4.4 %fusion.18 = bf16[8,512,128]{1,2,0:T(8,128)(2,1)S(1)} fusion(bf16[512,8,128]{0,2,1:T(8,128)(2,1)S(1)} %bitcast.99, f32[8,512,512]{1,2,0:T(8,128)} %get-tuple-element.27, f32[8,512]{1,0:T(8,128)S(1)} %get-tuple-element.26), kind=kOutput, calls=%fused_computation.25 | convolution fusion | flops 541589504 | bytes 10502144 | tf_op jit(solution)/shard_map/hqk,khe->qhe/dot_general | solution.py:362
  236.4 0.4 copy-done.7
  236.8 7.2 %convolution_convert_fusion = bf16[4096,1024]{1,0:T(8,128)(2,1)} fusion(bf16[4096,512]{1,0:T(8,128)(2,1)S(1)} %bitcast.91, bf16[512,1024]{0,1:T(8,128)(2,1)S(1)} %bitcast.104), kind=kOutput, calls=%fused_computation.6 | convolution fusion | flops 4299161600 | bytes 13631488 | tf_op jit(solution)/shard_map/btd,th->bdh/dot_general | solution.py:389
  244.0 0.0 reduce-scatter.3.cloned.1.call-update
  244.0 5.3 %multiply_reduce_fusion = (f32[8,512]{1,0:T(8,128)S(1)}, f32[8,512,512]{1,2,0:T(8,128)S(1)}) fusion(f32[8,512,512]{1,2,0:T(8,128)} %get-tuple-element.27, f32[8,512]{1,0:T(8,128)S(1)} %get-tuple-element.26, bf16[512,8,128]{0,2,1:T(8,128)(2,1)S(1)} %bitcast.100, bf16[64,8,8,128]{3,2,1,0:T(8,128)(2,1)} %fusion.21), kind=kOutput, calls=%fused_computation.3 | convolution fusion | flops 543158272 | bytes 18907136 | tf_op jit(solution)/shard_map/qhe,khe->hqk/dot_general | solution.py:363
  249.3 4.5 %multiply_convert_fusion = bf16[8,512,512]{1,2,0:T(8,128)(2,1)S(1)} fusion(f32[8,512,512]{1,2,0:T(8,128)S(1)} %get-tuple-element.29, f32[8,512]{1,0:T(8,128)S(1)} %get-tuple-element.28, f32[8,512,512]{1,2,0:T(8,128)} %get-tuple-element.27, f32[8,512]{1,0:T(8,128)S(1)} %get-tuple-element.26), kind=kLoop, calls=%fused_computation.2 | loop fusion | flops 8388608 | bytes 21004288 | tf_op jit(solution)/shard_map/convert_element_type | solution.py:365
  253.8 0.0 copy-start.6
  253.8 2.0 copy-done.6
  255.8 0.7 multiply_convert_fusion.2
  256.6 1.3 copy.73
  257.9 3.8 multiply_convert_fusion.1
  261.7 1.3 copy.74
  263.0 2.8 all-gather.6.cloned.1.call-done
  265.8 6.5 %copy.62 = bf16[512,8,512]{0,2,1:T(8,128)(2,1)} copy(bf16[512,8,512]{2,0,1:T(8,128)(2,1)} %all-gather.6.cloned.1.call-done) | data formatting | bytes 8388608 | tf_op jit(solution)/shard_map/all_gather | solution.py:398
  272.2 6.3 %copy.72 = bf16[1,512,4096]{2,1,0:T(8,128)(2,1)} copy(bf16[1,512,4096]{1,2,0:T(8,128)(2,1)} %bitcast.87) | data formatting | bytes 8388608
  278.6 39.4 %reduce-scatter.5.cloned.1.call-done = bf16[256,1024]{0,1:T(8,128)(2,1)} async-done(((bf16[4096,1024]{0,1:T(8,128)(2,1)}), bf16[256,1024]{0,1:T(8,128)(2,1)}) %reduce-scatter.5.cloned.1.call-update) | async-done | bytes 524304 | tf_op jit(solution)/shard_map/reduce_scatter | solution.py:385
  318.0 1.1 bitcast_convert_fusion.1
  319.1 1.3 copy.75
  320.4 98.0 %reduce-scatter.3.cloned.1.call-done = bf16[256,1024]{1,0:T(8,128)(2,1)} async-done(((bf16[4096,1024]{1,0:T(8,128)(2,1)}), bf16[256,1024]{1,0:T(8,128)(2,1)}) %reduce-scatter.3.cloned.1.call-update) | async-done | bytes 524304 | tf_op jit(solution)/shard_map/reduce_scatter | solution.py:385
  418.4 2.1 bitcast_convert_fusion.2
  (2 shorter events, 0.0 us)
Async XLA Ops:
  8.0 196.8 %all-gather.4.cloned.1.call-start = ((), (), s32[]{:S(2)}) async-start(), calls=%async_computation.2 | async-start | bytes 5242880 | tf_op jit(solution)/shard_map/all_gather | solution.py:393
  11.9 1.2 copy-start.1
  13.1 1.0 copy-start.2
  14.2 1.0 copy-start.3
  15.2 0.7 copy-start.4
  15.9 0.7 copy-start.5
  131.9 9.5 %copy-start = (bf16[4,512,1024]{2,1,0:T(8,128)(2,1)}, bf16[4,512,1024]{2,1,0:T(8,128)(2,1)S(1)}, u32[]{:S(2)}) copy-start(bf16[4,512,1024]{2,1,0:T(8,128)(2,1)S(1)} %get-tuple-element.8) | copy-start | bytes 12582916
  152.1 10.0 %copy-start.9 = (bf16[8,128,512]{2,1,0:T(8,128)(2,1)}, bf16[8,128,512]{2,1,0:T(8,128)(2,1)S(1)}, u32[]{:S(2)}) copy-start(bf16[8,128,512]{2,1,0:T(8,128)(2,1)S(1)} %fusion.15) | copy-start | bytes 3145732
  153.4 112.4 %all-gather.6.cloned.1.call-start = ((), (), s32[]{:S(2)}) async-start(), calls=%async_computation.5 | async-start | bytes 5242880 | tf_op jit(solution)/shard_map/all_gather | solution.py:398
  204.8 9.3 %copy-start.10 = (bf16[8,128,512]{2,1,0:T(8,128)(2,1)S(1)}, bf16[8,128,512]{2,1,0:T(8,128)(2,1)}, u32[]{:S(2)}) copy-start(bf16[8,128,512]{2,1,0:T(8,128)(2,1)} %copy-done.9) | copy-start | bytes 3145732
  214.1 103.9 %reduce-scatter.5.cloned.1.call-start = ((), (), s32[]{:S(2)}) async-start(), calls=%async_computation.4 | async-start | bytes 8912896 | tf_op jit(solution)/shard_map/reduce_scatter | solution.py:385
  223.0 1.3 copy-start.8
  223.0 195.4 %reduce-scatter.3.cloned.1.call-start = ((), (), s32[]{:S(2)}) async-start(), calls=%async_computation.3 | async-start | bytes 8912896 | tf_op jit(solution)/shard_map/reduce_scatter | solution.py:385
  225.6 6.4 %copy-start.11 = (bf16[1,512,1024]{1,2,0:T(8,128)(2,1)S(1)}, bf16[1,512,1024]{1,2,0:T(8,128)(2,1)}, u32[]{:S(2)}) copy-start(bf16[1,512,1024]{1,2,0:T(8,128)(2,1)} %copy.84) | copy-start | bytes 3145732
  232.0 4.7 %copy-start.7 = (bf16[4,1024,512]{2,1,0:T(8,128)(2,1)S(1)}, bf16[4,1024,512]{2,1,0:T(8,128)(2,1)}, u32[]{:S(2)}) copy-start(bf16[4,1024,512]{2,1,0:T(8,128)(2,1)} %copy.69) | copy-start | bytes 12582916
  253.8 2.0 copy-start.6
Sparse Core Ops, SparseCore 0:
  153.5 51.2 all-gather.3
  214.2 51.5 all-gather.5
Sparse Core Ops, SparseCore 1:
  223.1 94.8 reduce-scatter.4
  320.3 98.1 reduce-scatter.2

commit v2 on v1

--- a/solution.py
+++ b/solution.py
@@ -9,6 +9,8 @@
 
 HEAD_DIM = 128
 MESH = pl.DeviceIdType.MESH
+NT = (((1,), (1,)), ((), ()))
+TN = (((0,), (0,)), ((), ()))
 SLOTS = 48
 PAD = 64
 
@@ -134,13 +136,32 @@
     return first, second_y, second_x, third_step, fourth_step, last
 
 
+def attention_forward(head, query_ref, key_ref, value_ref, allowed, probs_ref, attended_ref):
+    lanes = pl.ds(pl.multiple_of(head * HEAD_DIM, HEAD_DIM), HEAD_DIM)
+    scores = lax.dot_general(key_ref[:, lanes], query_ref[:, lanes], NT, preferred_element_type=jnp.float32)
+    scores = jnp.where(allowed, scores * HEAD_DIM**-0.5, -1e30)
+    weights = jnp.exp(scores - jnp.max(scores, axis=0, keepdims=True))
+    probs = (weights / jnp.sum(weights, axis=0, keepdims=True)).astype(jnp.bfloat16)
+    probs_ref[head] = probs
+    attended = lax.dot_general(probs, value_ref[:, lanes], TN, preferred_element_type=jnp.float32)
+    attended_ref[:, lanes] = attended.astype(jnp.bfloat16)
+
+
 def relay_kernel(
-    tile_ref, target_ref, row_ref, wo_ref, vw_ref,
-    g_ref, wo_all, vw_all,
-    packed, places, landed, landed_places, spread, canvas, vw_own,
-    send_sem, recv_sem, data_send, data_recv, place_send, place_recv, share_send, share_recv, local_sem,
+    tile_hbm, target_ref, row_ref, wo_ref, vw_ref, query_hbm, key_hbm, value_hbm, position_ref,
+    g_ref, wo_all, vw_all, probs_ref, attended_ref,
+    tile_ref, query_ref, key_ref, value_ref, packed, places, landed, landed_places, spread, canvas, vw_own,
+    send_sem, recv_sem, data_send, data_recv, place_send, place_recv, share_send, share_recv, local_sem, load_sem,
 ):
     at = Place()
+    loads = [
+        pltpu.make_async_copy(src, dst, load_sem.at[k])
+        for k, (src, dst) in enumerate(
+            ((tile_hbm, tile_ref), (query_hbm, query_ref), (key_hbm, key_ref), (value_hbm, value_ref))
+        )
+    ]
+    for load in loads:
+        load.start()
     groups = 16
     tok = tile_ref.shape[0]
     barrier = greet(
@@ -162,6 +183,7 @@
     choose = jnp.where(
         lax.broadcasted_iota(jnp.int32, (groups * SLOTS, tok), 0) == slot, 1.0, 0.0
     ).astype(jnp.bfloat16)
+    loads[0].wait()
     packed[...] = jnp.dot(choose, tile_ref[...], preferred_element_type=jnp.float32).astype(jnp.bfloat16)
 
     lane = within + PAD * (at.w % 2)
@@ -171,9 +193,8 @@
     place = row_ref[...] + 1
     high = (place // 32).astype(jnp.float32)
     low = (place % 32).astype(jnp.float32)
-    nt = (((1,), (1,)), ((), ()))
-    high = lax.dot_general((member * high).astype(jnp.bfloat16), to_lane, nt, preferred_element_type=jnp.float32)
-    low = lax.dot_general((member * low).astype(jnp.bfloat16), to_lane, nt, preferred_element_type=jnp.float32)
+    high = lax.dot_general((member * high).astype(jnp.bfloat16), to_lane, NT, preferred_element_type=jnp.float32)
+    low = lax.dot_general((member * low).astype(jnp.bfloat16), to_lane, NT, preferred_element_type=jnp.float32)
     lanes = (high * 32.0 + low).astype(jnp.int32)
     places[...] = jnp.broadcast_to(lanes[:, None, :], places.shape)
     landed[:, SLOTS:, :] = jnp.zeros((groups, PAD - SLOTS, landed.shape[2]), landed.dtype)
@@ -238,12 +259,27 @@
     value_steps = gather_wide(at, links, vw_own, vw_all, local_sem.at[1])
     out_steps[0]()
 
+    key_at = lax.broadcasted_iota(jnp.int32, (tok, tok), 0)
+    query_at = lax.broadcasted_iota(jnp.int32, (tok, tok), 1)
+    earliest = lax.broadcasted_iota(jnp.int32, (1, tok), 1) - position_ref[...]
+
+    def heads(first, last):
+        @pl.loop(first, last)
+        def _(head):
+            allowed = (key_at <= query_at) & (key_at >= earliest)
+            attention_forward(head, query_ref, key_ref, value_ref, allowed, probs_ref, attended_ref)
+
+    for load in loads[1:]:
+        load.wait()
+    heads(0, 2)
+
     for b in range(4):
         piece = vw_own.at[pl.ds(b * half_chunk, half_chunk)]
         pltpu.make_async_copy(piece, piece, share_recv.at[b]).wait()
     value_steps[0]()
     out_steps[1]()
     out_steps[2]()
+    heads(2, 5)
 
     @pl.loop(0, groups)
     def _(i):
@@ -272,6 +308,7 @@
     value_steps[1]()
     value_steps[2]()
     out_steps[4]()
+    heads(5, 8)
 
     first, second = pl.ds(0, part), pl.ds(part, part)
     z_p[0].wait_recv()
@@ -308,7 +345,7 @@
     links.drain()
 
 
-def relay_and_gather(tile, target, row, wo, vw):
+def relay_and_gather(tile, target, row, wo, vw, query, key, value, position):
     tok, width = tile.shape
     bf16 = jnp.bfloat16
     dma = pltpu.SemaphoreType.DMA
@@ -321,10 +358,13 @@
             jax.ShapeDtypeStruct((4, tok, width), bf16),
             jax.ShapeDtypeStruct((16,) + wo.shape, bf16),
             jax.ShapeDtypeStruct((16,) + vw.shape, bf16),
+            jax.ShapeDtypeStruct((width // HEAD_DIM, tok, tok), bf16),
+            jax.ShapeDtypeStruct((tok, width), bf16),
         ),
-        in_specs=[vmem] * 5,
-        out_specs=(hbm, hbm, hbm),
+        in_specs=[hbm, vmem, vmem, hbm, hbm, hbm, hbm, hbm, vmem],
+        out_specs=(hbm, hbm, hbm, vmem, vmem),
         scratch_shapes=[
+            *[pltpu.VMEM((tok, width), bf16)] * 4,
             pltpu.VMEM((16 * SLOTS, width), bf16),
             pltpu.VMEM((16, 8, 128), jnp.int32),
             pltpu.VMEM((16, PAD, width), bf16),
@@ -334,68 +374,397 @@
             pltpu.VMEM(vw.shape, bf16),
             dma((copies,)), dma((copies,)),
             dma((16,)), dma((16,)), dma((16,)), dma((16,)),
-            dma((4,)), dma((4,)), dma((3,)),
+            dma((4,)), dma((4,)), dma((3,)), dma((4,)),
         ],
         compiler_params=pltpu.CompilerParams(
-            collective_id=0, has_side_effects=True, vmem_limit_bytes=40 * 1024 * 1024
+            collective_id=0, has_side_effects=True, vmem_limit_bytes=60 * 1024 * 1024
         ),
         name="relay_and_gather",
-    )(tile, target, row, wo, vw)
-
-
-def attention_backward(query_rows, key_rows, value_rows, position_rows, grad_attended):
-    tok_rows = query_rows.shape[0]
-    heads_here = query_rows.shape[1] // HEAD_DIM
-    scale = HEAD_DIM ** (-0.5)
-    query_heads = query_rows.reshape(tok_rows, heads_here, HEAD_DIM)
-    key_heads = key_rows.reshape(tok_rows, heads_here, HEAD_DIM)
-    value_heads = value_rows.reshape(tok_rows, heads_here, HEAD_DIM)
-    gout_heads = grad_attended.reshape(tok_rows, heads_here, HEAD_DIM)
-    index = jnp.arange(tok_rows, dtype=jnp.int32)
-    allowed = (index[None, :] <= index[:, None]) & (index[None, :] >= (index - position_rows)[:, None])
-    f32 = dict(preferred_element_type=jnp.float32)
-    scores = jnp.einsum("qhe,khe->hqk", query_heads, key_heads, **f32) * scale
-    scores = jnp.where(allowed[None], scores, -1e30)
-    weights = jnp.exp(scores - jnp.max(scores, axis=-1, keepdims=True))
-    probs = weights / jnp.sum(weights, axis=-1, keepdims=True)
-    probs_low = probs.astype(jnp.bfloat16)
-    attended = jnp.einsum("hqk,khe->qhe", probs_low, value_heads, **f32).astype(jnp.bfloat16)
-    dprob = jnp.einsum("qhe,khe->hqk", gout_heads, value_heads, **f32)
-    delta = jnp.sum(probs * dprob, axis=-1, keepdims=True)
-    dscore = (probs * (dprob - delta)).astype(jnp.bfloat16)
-    grad_value = jnp.einsum("hqk,qhe->khe", probs_low, gout_heads, **f32).astype(jnp.bfloat16)
-    grad_key = (jnp.einsum("hqk,qhe->khe", dscore, query_heads, **f32) * scale).astype(jnp.bfloat16)
-    grad_query = (jnp.einsum("hqk,khe->qhe", dscore, key_heads, **f32) * scale).astype(jnp.bfloat16)
-    flat = (tok_rows, heads_here * HEAD_DIM)
-    return tuple(a.reshape(flat) for a in (attended, grad_value, grad_query, grad_key))
+    )(tile, target, row, wo, vw, query, key, value, position)
+
+
+def scatter_wide(at, links, mine, from_y, via, from_x, result):
+    half = result.shape[0] // 2
+    quarter = half // 2
+    lower, upper = pl.ds(0, half), pl.ds(half, half)
+    xp, xm, yy = (at.wide(w) for w in (at.w_xp, at.w_xm, at.w_y))
+    ya, yb = from_y
+    state = {}
+
+    def add(dx, dy, rows, *others):
+        ref = mine(dx, dy).at[rows]
+        total = ref[...].astype(jnp.float32)
+        for other in others:
+            total = total + other[...].astype(jnp.float32)
+        return ref, total
+
+    def add_into(dx, dy, rows, *others):
+        ref, total = add(dx, dy, rows, *others)
+        ref[...] = total.astype(jnp.bfloat16)
+
+    def across(name, slot, dx_dy, start):
+        for k, device in ((0, xp), (1, xm)):
+            rows = pl.ds(start + k * quarter, quarter)
+            state[name, k] = links.put(mine(*dx_dy).at[rows], via.at[slot, k], device)
+
+    def first_a():
+        state["ya2"] = links.put(mine(2, 1).at[lower], ya.at[2], yy)
+        across("vb1", 1, (2, 1), half)
+        across("vb0", 0, (2, 0), half)
+
+    def first_b():
+        for dx in (1, 3, 0):
+            state["ya%d" % dx] = links.put(mine(dx, 1).at[lower], ya.at[dx], yy)
+
+    def onward(name, slot, dy, start, rows):
+        for k, dx, device in ((0, 1, xp), (1, 3, xm)):
+            state[name, k].wait_recv()
+            add_into(dx, dy, pl.ds(start + k * quarter, quarter), via.at[slot, k])
+            state["r" + name, k] = links.put(mine(dx, dy).at[rows], from_x.at[slot, k], device)
+
+    def second():
+        state["ya2"].wait_recv()
+        add_into(2, 0, lower, ya.at[2])
+        across("va", 2, (2, 0), 0)
+        onward("vb1", 1, 1, half, upper)
+        onward("vb0", 0, 0, half, upper)
+
+    def third():
+        for dx in (1, 3):
+            state["ya%d" % dx].wait_recv()
+            add_into(dx, 0, lower, ya.at[dx])
+        onward("va", 2, 0, 0, lower)
+        for k in range(2):
+            state["rvb1", k].wait_recv()
+        add_into(0, 1, upper, from_x.at[1, 0], from_x.at[1, 1])
+        state["yb"] = links.put(mine(0, 1).at[upper], yb, yy)
+
+    def fourth():
+        state["ya0"].wait_recv()
+        for k in range(2):
+            state["rva", k].wait_recv()
+        result[lower, :] = add(0, 0, lower, ya.at[0], from_x.at[2, 0], from_x.at[2, 1])[1]
+        for k in range(2):
+            state["rvb0", k].wait_recv()
+        state["yb"].wait_recv()
+        result[upper, :] = add(0, 0, upper, yb, from_x.at[0, 0], from_x.at[0, 1])[1]
+
+    return first_a, first_b, second, third, fourth
+
+
+def backward_kernel(
+    g_hbm, attended_hbm, query_hbm, key_hbm, value_hbm, wo_hbm, vw_hbm, probs_hbm, normed_hbm,
+    gin_hbm, gq_ref, gk_ref, gow_ref, gvw_ref,
+    g_ref, attended_ref, query_ref, key_ref, value_ref, weight, other, out_mine, core_out, core_value, ya_out, yb_out, via_out, x_out, ya_val, yb_val, via_val, x_val,
+    gv_own, gv_all, probs, vw_tiles, stage,
+    send_sem, recv_sem, core_send, core_recv, gv_send, gv_recv, gin_send, gin_recv, local_sem, probs_sem, tile_sem, own_sem, g_sem,
+):
+    at = Place()
+    tok, width = attended_hbm.shape
+    rows = gow_ref.shape[0]
+    links = Links(send_sem, recv_sem)
+    barrier = greet(
+        [at.wide(w) for w in (at.w_xp, at.w_xm, at.w_y, at.w_core)] + [at.narrow(n) for n in (at.n_p, at.n_m)]
+    )
+    load_g = [
+        pltpu.make_async_copy(g_hbm.at[pl.ds(b, 1)], g_ref.at[pl.ds(b, 1)], g_sem.at[b]) for b in range(4)
+    ]
+    load_g.append(pltpu.make_async_copy(attended_hbm, attended_ref, g_sem.at[4]))
+    for load in load_g:
+        load.start()
+    load_rest = [
+        pltpu.make_async_copy(src, dst, local_sem.at[k])
+        for k, (src, dst) in enumerate(
+            ((query_hbm, query_ref), (key_hbm, key_ref), (value_hbm, value_ref), (wo_hbm, weight))
+        )
+    ]
+    for load in load_rest:
+        load.start()
+
+    def load_probs(pair):
+        return pltpu.make_async_copy(probs_hbm.at[pl.ds(2 * pair, 2)], probs.at[pair % 2], probs_sem.at[pair % 2])
+
+    load_probs(0).start()
+
+    def chip(dx, dy):
+        y = at.y if dy == 0 else 1 - at.y
+        return ((at.x + dx) % 4) * 2 + y
+
+    def chip_of(i):
+        dx = (2 + i // 2) % 4
+        y = (at.y + 1 + i) % 2
+        return (at.x + dx) % 4, y
+
+    pl.semaphore_wait(barrier, 6)
+
+    def terms(which, left, right, to_core, mine, landing):
+        def send(i):
+            x, y = chip_of(i)
+            return pltpu.make_async_remote_copy(
+                src_ref=to_core(x, y), dst_ref=landing.at[x * 2 + y],
+                send_sem=core_send.at[which, i], recv_sem=core_recv.at[which, i],
+                device_id=at.wide(at.w_core), device_id_type=MESH,
+            )
+
+        def theirs():
+            @pl.loop(0, 8)
+            def _(i):
+                x, y = chip_of(i)
+                term = lax.dot_general(left(x, y, 1 - at.core), right[...], TN, preferred_element_type=jnp.float32)
+                to_core(x, y)[...] = term.astype(jnp.bfloat16)
+                send(i).start()
+
+        def ours(first, last):
+            @pl.loop(first, last)
+            def _(i):
+                x, y = chip_of(i)
+                term = lax.dot_general(left(x, y, at.core), right[...], TN, preferred_element_type=jnp.float32)
+                send(i).wait_recv()
+                term = term + landing[x * 2 + y].astype(jnp.float32)
+                mine(x * 2 + y)[...] = term.astype(jnp.bfloat16)
+
+        def drain():
+            @pl.loop(0, 8)
+            def _(i):
+                send(i).wait_send()
+
+        return theirs, ours, drain
+
+    def g_columns(x, y, core):
+        return g_ref[x, :, pl.ds(pl.multiple_of(y * 512 + core * 256, 256), 256)]
+
+    def normed_columns(x, y, core):
+        return other[:, pl.ds(pl.multiple_of(x * 1024 + y * 512 + core * 256, 256), 256)]
+
+    def in_other(x, y):
+        return other.at[pl.ds(pl.multiple_of(y * 256, 256), 256), pl.ds(pl.multiple_of(x * 1024, 1024), 1024)]
+
+    theirs, ours, drain_core = terms(0, g_columns, attended_ref, in_other, lambda j: out_mine.at[j], core_out)
+    out_steps = scatter_wide(
+        at, links, lambda dx, dy: out_mine.at[chip(dx, dy)], (ya_out, yb_out), via_out, x_out, gow_ref
+    )
+    for load in load_g:
+        load.wait()
+    theirs()
+    ours(0, 2)
+    out_steps[0]()
+    ours(2, 8)
+    out_steps[1]()
+    drain_core()
+    load_normed = pltpu.make_async_copy(normed_hbm, other, local_sem.at[4])
+    load_normed.start()
+    for load in load_rest:
+        load.wait()
+
+    part = tok // 2
+    scale = HEAD_DIM**-0.5
+
+    def gv_copies(pair):
+        def copy(k, src, device):
+            return pltpu.make_async_remote_copy(
+                src_ref=src, dst_ref=src, send_sem=gv_send.at[k, pair], recv_sem=gv_recv.at[k, pair],
+                device_id=at.narrow(device), device_id_type=MESH,
+            )
+
+        mine = gv_all.at[at.n, pair]
+        on_p = gv_all.at[at.n_m, pair, pl.ds(0, part)]
+        on_m = gv_all.at[at.n_p, pair, pl.ds(part, part)]
+        return copy(0, mine, at.n_p), copy(1, mine, at.n_m), copy(2, on_p, at.n_p), copy(3, on_m, at.n_m)
+
+    def forward_gv(pair):
+        to_p, to_m, on_p, on_m = gv_copies(pair)
+        to_p.wait_recv()
+        on_p.start()
+        to_m.wait_recv()
+        on_m.start()
+
+    def attend(pair):
+        lanes = pl.ds(pair * 256, 256)
+        load_probs(pair).wait()
+        if pair < 3:
+            load_probs(pair + 1).start()
+        total = jnp.zeros((tok, 256), jnp.float32)
+        for b in range(4):
+            block = weight[4 * b : 4 * b + 4, :, lanes].reshape(width, 256)
+            total = total + jnp.dot(g_ref[b], block, preferred_element_type=jnp.float32)
+        both = total.astype(jnp.bfloat16)
+        for h in range(2):
+            cols = pl.ds(pair * 256 + h * HEAD_DIM, HEAD_DIM)
+            gout = both[:, h * HEAD_DIM : (h + 1) * HEAD_DIM]
+            prob = probs[pair % 2, h]
+            dprob = lax.dot_general(value_ref[:, cols], gout, NT, preferred_element_type=jnp.float32)
+            wide_prob = prob.astype(jnp.float32)
+            delta = jnp.sum(wide_prob * dprob, axis=0, keepdims=True)
+            dscore = (wide_prob * (dprob - delta)).astype(jnp.bfloat16)
+            gv = jnp.dot(prob, gout, preferred_element_type=jnp.float32).astype(jnp.bfloat16)
+            gv_own[:, cols] = gv
+            gv_all[at.n, pair, :, pl.ds(h * HEAD_DIM, HEAD_DIM)] = gv
+            gk = jnp.dot(dscore, query_ref[:, cols], preferred_element_type=jnp.float32) * scale
+            gk_ref[:, cols] = gk.astype(jnp.bfloat16)
+            gq = lax.dot_general(dscore, key_ref[:, cols], TN, preferred_element_type=jnp.float32) * scale
+            gq_ref[:, cols] = gq.astype(jnp.bfloat16)
+        to_p, to_m, _, _ = gv_copies(pair)
+        to_p.start()
+        to_m.start()
+        if pair > 0:
+            forward_gv(pair - 1)
+
+    attend(0)
+    attend(1)
+    out_steps[2]()
+    attend(2)
+    attend(3)
+    out_steps[3]()
+
+    def load_tile(tile):
+        return pltpu.make_async_copy(vw_hbm.at[pl.ds(4 * tile, 4)], vw_tiles.at[tile % 2], tile_sem.at[tile % 2])
+
+    load_tile(0).start()
+    load_tile(1).start()
+    load_normed.wait()
+    theirs, ours, drain_value = terms(
+        1, normed_columns, gv_own, lambda x, y: weight.at[x * 2 + y], lambda j: weight.at[8 + j], core_value
+    )
+    value_steps = scatter_wide(
+        at, links, lambda dx, dy: weight.at[8 + chip(dx, dy)], (ya_val, yb_val), via_val, x_val, gvw_ref
+    )
+    theirs()
+    forward_gv(3)
+    ours(0, 2)
+    value_steps[0]()
+    ours(2, 8)
+    value_steps[1]()
+
+    for pair in range(4):
+        _, _, on_p, on_m = gv_copies(pair)
+        on_p.wait_recv()
+        on_m.wait_recv()
+
+    def gin_copies(tile, y):
+        def copy(k, src, dst, device):
+            return pltpu.make_async_remote_copy(
+                src_ref=src, dst_ref=dst, send_sem=gin_send.at[k, 2 * tile + y], recv_sem=gin_recv.at[k, 2 * tile + y],
+                device_id=at.narrow(device), device_id_type=MESH,
+            )
+
+        def chunk(n, start, size):
+            cols = pl.ds(pl.multiple_of(tile * 1024 + y * 512 + n * 128, 128), 128)
+            return gin_hbm.at[pl.ds(start, size), cols]
+
+        src, dst = stage.at[tile, :, pl.ds(y * 128, 128)], chunk(at.n, 0, tok)
+        on_p, on_m = chunk(at.n_m, 0, part), chunk(at.n_p, part, part)
+        own = pltpu.make_async_copy(src, dst, own_sem.at[2 * tile + y])
+        return copy(0, src, dst, at.n_p), copy(1, src, dst, at.n_m), copy(2, on_p, on_p, at.n_p), copy(3, on_m, on_m, at.n_m), own
+
+    def forward_gin(tile):
+        for y in range(2):
+            to_p, to_m, on_p, on_m, _ = gin_copies(tile, y)
+            to_p.wait_recv()
+            on_p.start()
+            to_m.wait_recv()
+            on_m.start()
+
+    for tile in range(4):
+        load_tile(tile).wait()
+        chunk = pl.multiple_of(at.n * 128, 128)
+        low = g_ref[tile, :, pl.ds(chunk, 128)]
+        high = g_ref[tile, :, pl.ds(pl.multiple_of(chunk + 512, 128), 128)]
+        total = jnp.concatenate([low, high], axis=1).astype(jnp.float32)
+        for z in range(4):
+            for pair in range(4):
+                block = vw_tiles[tile % 2, :, z * 64 : (z + 1) * 64, pair * 256 : (pair + 1) * 256].reshape(256, 256)
+                total = total + lax.dot_general(gv_all[z, pair], block, NT, preferred_element_type=jnp.float32)
+        stage[tile] = total.astype(jnp.bfloat16)
+        for y in range(2):
+            to_p, to_m, _, _, own = gin_copies(tile, y)
+            to_p.start()
+            to_m.start()
+            own.start()
+        if tile < 2:
+            load_tile(tile + 2).start()
+
+    out_steps[4]()
+    value_steps[2]()
+    forward_gin(0)
+    forward_gin(1)
+    value_steps[3]()
+    forward_gin(2)
+    forward_gin(3)
+    value_steps[4]()
+    drain_value()
+    for tile in range(4):
+        for y in range(2):
+            to_p, to_m, on_p, on_m, own = gin_copies(tile, y)
+            on_p.wait_recv()
+            on_m.wait_recv()
+            own.wait()
+            for copy in (to_p, to_m, on_p, on_m):
+                copy.wait_send()
+        for copy in gv_copies(tile):
+            copy.wait_send()
+    links.drain()
+
+
+def backward_and_scatter(full_grad, attended, query, key, value, out_all, value_all, probs, normed):
+    _, tok, width = full_grad.shape
+    rows = out_all.shape[1]
+    bf16, f32 = jnp.bfloat16, jnp.float32
+    dma = pltpu.SemaphoreType.DMA
+    vmem = pl.BlockSpec(memory_space=pltpu.VMEM)
+    hbm = pl.BlockSpec(memory_space=pl.ANY)
+    half = rows // 2
+    landing = [
+        pltpu.VMEM((4, half, width), bf16),
+        pltpu.VMEM((half, width), bf16),
+        pltpu.VMEM((3, 2, half // 2, width), bf16),
+        pltpu.VMEM((3, 2, half, width), bf16),
+    ]
+    copies = 34
+    return pl.pallas_call(
+        backward_kernel,
+        out_shape=(
+            jax.ShapeDtypeStruct((tok, 4 * width), bf16),
+            jax.ShapeDtypeStruct((tok, width), bf16),
+            jax.ShapeDtypeStruct((tok, width), bf16),
+            jax.ShapeDtypeStruct((rows, width), f32),
+            jax.ShapeDtypeStruct((rows, width), f32),
+        ),
+        in_specs=[hbm] * 9,
+        out_specs=(hbm, vmem, vmem, vmem, vmem),
+        scratch_shapes=[
+            pltpu.VMEM((4, tok, width), bf16),
+            *[pltpu.VMEM((tok, width), bf16)] * 4,
+            pltpu.VMEM((16, rows, width), bf16),
+            pltpu.VMEM((tok, 4 * width), bf16),
+            pltpu.VMEM((8, rows, width), bf16),
+            pltpu.VMEM((8, rows, width), bf16),
+            pltpu.VMEM((8, rows, width), bf16),
+            *landing,
+            *landing,
+            pltpu.VMEM((tok, width), bf16),
+            pltpu.VMEM((4, 4, tok, 256), bf16),
+            pltpu.VMEM((2, 2, tok, tok), bf16),
+            pltpu.VMEM((2, 4, rows, width), bf16),
+            pltpu.VMEM((4, tok, 256), bf16),
+            dma((copies,)), dma((copies,)),
+            dma((2, 8)), dma((2, 8)),
+            dma((4, 4)), dma((4, 4)), dma((4, 8)), dma((4, 8)),
+            dma((5,)), dma((2,)), dma((2,)), dma((8,)), dma((5,)),
+        ],
+        compiler_params=pltpu.CompilerParams(
+            collective_id=1, has_side_effects=True, vmem_limit_bytes=62 * 1024 * 1024
+        ),
+        name="backward_and_scatter",
+    )(full_grad, attended, query, key, value, out_all, value_all, probs, normed)
 
 
 def shards(boundary_grad, tile_target, tile_row, normed_input, query, keys, values, positions, out_weight, value_weight):
-    f32 = dict(preferred_element_type=jnp.float32)
-    full_grad, out_all, value_all = relay_and_gather(
-        boundary_grad[0], tile_target, tile_row, out_weight[0], value_weight[0]
+    full_grad, out_all, value_all, probs, attended = relay_and_gather(
+        boundary_grad[0], tile_target, tile_row, out_weight[0], value_weight[0], query[0], keys[0], values[0], positions
     )
-    tok, width = full_grad.shape[1:]
-    grad_attended = jnp.einsum("btd,bdh->th", full_grad, out_all.reshape(4, width, width), **f32).astype(jnp.bfloat16)
-    attended, grad_value, grad_query, grad_key = attention_backward(
-        query[0], keys[0], values[0], positions[0], grad_attended
+    grad_input, grad_query, grad_key, grad_out_weight, grad_value_weight = backward_and_scatter(
+        full_grad, attended, query[0], keys[0], values[0], out_all, value_all, probs, normed_input[0]
     )
-
-    def scattered(term):
-        return lax.psum_scatter(
-            term.astype(jnp.bfloat16), "wide", scatter_dimension=0, tiled=True
-        ).astype(jnp.float32)
-
-    out_term = jnp.einsum("btd,th->bdh", full_grad, attended, **f32).reshape(4 * width, width)
-    grad_out_weight = scattered(out_term)
-    value_term = jnp.einsum("td,th->dh", normed_input[0], grad_value, **f32)
-    grad_value_weight = scattered(value_term)
-    gv_all = lax.all_gather(grad_value, "narrow", axis=0)
-    piece = jnp.einsum("btk,jcbik->tjci", gv_all, value_all.reshape(8, 2, 4, 64, width), **f32).reshape(tok, 8, 128)
-    whole = jnp.transpose(full_grad, (1, 0, 2)).reshape(tok, 8, 4, 128)
-    mine = lax.dynamic_slice_in_dim(whole, lax.axis_index("narrow"), 1, 2)[:, :, 0]
-    piece = (mine.astype(jnp.float32) + piece).astype(jnp.bfloat16)
-    grad_input = lax.all_gather(piece, "narrow", axis=2).reshape(tok, 4 * width)
     return (grad_input[None], grad_query[None], grad_key[None], grad_out_weight[None], grad_value_weight[None])
 
 

time: 432 us -> 227 us (0.53)
  waiting for transfers between devices: 174 us -> 0 us
  Pallas kernels: 115 us -> 215 us
  matrix products: 59.6 us -> 0 us
  local copies, waits for them, and re-layouts: 54.3 us -> 8.74 us
  between operations: 15.6 us -> 0.67 us
  other arithmetic: 8.59 us -> 0 us
    reduce_scatter x2 -> x0, waiting for transfers between devices: 137 us -> none  [scattered(): lax.psum_scatter(term.astype(jnp.bfloat16), 'wide', scatter_dimension=0,...]
    pallas_call x0 -> x1, Pallas kernels: none -> 96.1 us  [backward_and_scatter(): pl.pallas_call(backward_kernel, out_shape=(jax.ShapeDtypeStruct((tok, 4 *...]
    dot_general x9 -> x0, matrix products: 54.2 us -> none  [the longest x1 9.52 us: shards(): jnp.einsum('btd,bdh->th', full_grad, out_all.reshape(4, width, width), **...]
    all_gather x2 -> x0, waiting for transfers between devices: 36.4 us -> none  [the longest x1 33.7 us: shards(): gv_all = lax.all_gather(grad_value, 'narrow', axis=0)]
    dot_general x2 -> x0, local copies, waits for them, and re-layouts: 14.8 us -> none  [the longest x1 8.4 us: shards(): jnp.einsum('btk,jcbik->tjci', gv_all, value_all.reshape(8, 2, 4, 64, widt...]
    unnamed x29 -> x13, local copies, waits for them, and re-layouts: 19.6 us -> 8.74 us
    all_gather x1 -> x0, local copies, waits for them, and re-layouts: 6.46 us -> none  [shards(): grad_input = lax.all_gather(piece, 'narrow', axis=2).reshape(tok, 4 * width)]
    transpose x1 -> x0, local copies, waits for them, and re-layouts: 6.38 us -> none  [shards(): whole = jnp.transpose(full_grad, (1, 0, 2)).reshape(tok, 8, 4, 128)]
  transfers between devices with their start and end apart: 4 -> 0, of which waited for: 4 -> 0; matrix products, arithmetic and copies ran while one was open for 18% -> 0% of each run, Pallas kernels for 0% -> 0%
where the time goes in v2:
time: 227 us; the launch traced here: 224 us
  Pallas kernels  215 us (95%)
  local copies, waits for them, and re-layouts  8.74 us (4%)
    pallas_call x1, Pallas kernels, relay_and_gather(): pl.pallas_call(relay_kernel, out_shape=(jax.ShapeDtypeStruct((4, tok, wid...  118 us
    pallas_call x1, Pallas kernels, backward_and_scatter(): pl.pallas_call(backward_kernel, out_shape=(jax.ShapeDtypeStruct((tok, 4 *...  96.1 us
    unnamed x13, local copies, waits for them, and re-layouts  8.74 us

profile of v2, /device:TPU:27, one launch (start us, length us, event | category | flops | bytes accessed | tf_op | source)
XLA Modules:
  0.0 224.0 jit_solution(4018709200067508916)
XLA Ops:
  0.6 118.4 %relay_and_gather.1 = (bf16[4,512,1024]{2,1,0:T(8,128)(2,1)}, bf16[16,256,1024]{2,1,0:T(8,128)(2,1)}, bf16[16,256,1024]{2,1,0:T(8,128)(2,1)}, bf16[8,512,512]{2,1,0:T(8,128)(2,1)}, bf16[512,1024]{1,0:T(8,128)(2,1)}) custom-call(bf16[512,1024]{1,0:T(8,128)(2,1)} %bitcast.24, s32[1,512]{1,0:T(1,128)} %target_ref.1, s32[1,512]{1,0:T(1,128)} %row_ref.1, ...), custom_call_target="tpu_custom_call" | custom-call | tf_op jit(solution)/shard_map/relay_and_gather/pallas_call | solution.py:355
  119.1 96.1 %backward_and_scatter.1 = (bf16[512,4096]{1,0:T(8,128)(2,1)}, bf16[512,1024]{1,0:T(8,128)(2,1)}, bf16[512,1024]{1,0:T(8,128)(2,1)}, f32[256,1024]{1,0:T(8,128)}, f32[256,1024]{1,0:T(8,128)}) custom-call(bf16[4,512,1024]{2,1,0:T(8,128)(2,1)} %get-tuple-element.15.g_hbm, bf16[512,1024]{1,0:T(8,128)(2,1)} %get-tuple-element.16.attended_hbm, ...), custom_call_target="tpu_custom_call" | custom-call | tf_op jit(solution)/shard_map/backward_and_scatter/pallas_call | solution.py:723
  215.2 0.0 copy-start.3
  215.2 0.0 copy-start.2
  215.2 4.8 %copy.20 = bf16[1,512,4096]{2,1,0:T(8,128)(2,1)} copy(bf16[1,512,4096]{2,1,0:T(8,128)(2,1)} %bitcast.12) | data formatting | bytes 8388608
  220.1 0.0 copy-done.3
  220.1 0.0 copy-start.1
  220.1 0.0 copy-start
  220.1 1.0 copy.21
  221.0 0.0 copy-done.2
  221.0 1.0 copy.22
  222.0 0.0 copy-done.1
  222.0 1.0 copy.23
  223.0 0.0 copy-done
  223.0 1.0 copy.24
Async XLA Ops:
  215.2 4.9 %copy-start.3 = (bf16[512,1024]{1,0:T(8,128)(2,1)S(1)}, bf16[512,1024]{1,0:T(8,128)(2,1)}, u32[]{:S(2)}) copy-start(bf16[512,1024]{1,0:T(8,128)(2,1)} %get-tuple-element.21) | copy-start | bytes 3145732
  215.2 5.8 %copy-start.2 = (bf16[512,1024]{1,0:T(8,128)(2,1)S(1)}, bf16[512,1024]{1,0:T(8,128)(2,1)}, u32[]{:S(2)}) copy-start(bf16[512,1024]{1,0:T(8,128)(2,1)} %get-tuple-element.22) | copy-start | bytes 3145732
  220.1 1.9 copy-start.1
  220.1 2.9 %copy-start = (f32[256,1024]{1,0:T(8,128)S(1)}, f32[256,1024]{1,0:T(8,128)}, u32[]{:S(2)}) copy-start(f32[256,1024]{1,0:T(8,128)} %get-tuple-element.24) | copy-start | bytes 3145732

commit v3 on v2

v3 whole, which is shorter than its diff:
```python
import functools

import jax
import jax.numpy as jnp
from jax import lax
from jax.experimental import pallas as pl
from jax.experimental.pallas import tpu as pltpu
from jax.sharding import PartitionSpec as P

HEAD_DIM = 128
MESH = pl.DeviceIdType.MESH
NT = (((1,), (1,)), ((), ()))
TN = (((0,), (0,)), ((), ()))
SLOTS = 48
PAD = 64


class Place:
    def __init__(self):
        self.s = lax.axis_index("section")
        self.w = lax.axis_index("wide")
        self.n = lax.axis_index("narrow")
        self.core = self.w % 2
        self.y = (self.w // 2) % 2
        self.x = self.w // 4
        self.w_xp = (self.w + 4) % 16
        self.w_xm = (self.w + 12) % 16
        self.w_x2 = (self.w + 8) % 16
        self.w_y = self.w + 2 - 4 * self.y
        self.w_core = self.w + 1 - 2 * self.core
        self.y_xp = (self.w_y + 4) % 16
        self.y_xm = (self.w_y + 12) % 16
        self.y_x2 = (self.w_y + 8) % 16
        self.n_p = (self.n + 1) % 4
        self.n_m = (self.n + 3) % 4
        self.n_2 = (self.n + 2) % 4

    def wide(self, w):
        return (self.s, w, self.n)

    def narrow(self, n):
        return (self.s, self.w, n)


class Links:
    def __init__(self, send_sem, recv_sem):
        self.send_sem, self.recv_sem, self.count, self.sent = send_sem, recv_sem, 0, []

    def put(self, src, dst, device):
        copy = pltpu.make_async_remote_copy(
            src_ref=src,
            dst_ref=dst,
            send_sem=self.send_sem.at[self.count],
            recv_sem=self.recv_sem.at[self.count],
            device_id=device,
            device_id_type=MESH,
        )
        copy.start()
        self.count += 1
        self.sent.append(copy)
        return copy

    def drain(self):
        for copy in self.sent:
            copy.wait_send()


def greet(devices):
    barrier = pltpu.get_barrier_semaphore()
    for device in devices:
        pl.semaphore_signal(barrier, inc=1, device_id=device, device_id_type=MESH)
    return barrier


def gather_wide(at, links, own, full, local_sem):
    half = own.shape[0] // 2
    lower, upper = pl.ds(0, half), pl.ds(half, half)
    third, fourth = pl.ds(half, half // 2), pl.ds(half + half // 2, half // 2)
    xp, xm, yy, cc = (at.wide(w) for w in (at.w_xp, at.w_xm, at.w_y, at.w_core))

    def send(w, device, rows=None):
        ref = full.at[w] if rows is None else full.at[w, rows]
        return links.put(ref, ref, device)

    state = {}

    def first():
        state["own"] = pltpu.make_async_copy(own, full.at[at.w], local_sem)
        state["own"].start()
        state["y"] = links.put(own, full.at[at.w], yy)
        state["xp"] = links.put(own, full.at[at.w], xp)
        state["xm"] = links.put(own, full.at[at.w], xm)
        state["core"] = links.put(own, full.at[at.w], cc)

    def second_y():
        state["y"].wait_recv()
        state["b_p"] = send(at.w_y, xp, upper)
        state["b_m"] = send(at.w_y, xm, upper)
        state["c_y"] = send(at.w_y, cc)

    def second_x():
        state["xp"].wait_recv()
        state["f_p"] = send(at.w_xm, xp, lower)
        state["g_m"] = send(at.w_xm, yy, lower)
        state["c_m"] = send(at.w_xm, cc)
        state["xm"].wait_recv()
        state["f_m"] = send(at.w_xp, xm, upper)
        state["g_p"] = send(at.w_xp, yy, lower)
        state["c_p"] = send(at.w_xp, cc)

    def third_step():
        state["b_p"].wait_recv()
        state["h_p"] = send(at.y_xm, xp, third)
        state["b_m"].wait_recv()
        state["h_m"] = send(at.y_xp, xm, fourth)
        state["f_p"].wait_recv()
        state["g_2"] = send(at.w_x2, yy, lower)
        state["f_m"].wait_recv()
        state["c_2"] = send(at.w_x2, cc)

    def fourth_step():
        state["g_m"].wait_recv()
        state["e_m"] = send(at.y_xm, cc)
        state["g_p"].wait_recv()
        state["e_p"] = send(at.y_xp, cc)
        state["h_p"].wait_recv()
        state["h_m"].wait_recv()
        state["g_2"].wait_recv()
        state["e_2"] = send(at.y_x2, cc)

    def last():
        state["own"].wait()
        for name in ("core", "c_y", "c_m", "c_p", "c_2", "e_m", "e_p", "e_2"):
            state[name].wait_recv()

    return first, second_y, second_x, third_step, fourth_step, last


def attention_forward(head, query_ref, key_ref, value_ref, allowed, probs_ref, attended_ref):
    lanes = pl.ds(pl.multiple_of(head * HEAD_DIM, HEAD_DIM), HEAD_DIM)
    scores = lax.dot_general(key_ref[:, lanes], query_ref[:, lanes], NT, preferred_element_type=jnp.float32)
    scores = jnp.where(allowed, scores * HEAD_DIM**-0.5, -1e30)
    weights = jnp.exp(scores - jnp.max(scores, axis=0, keepdims=True))
    probs = (weights / jnp.sum(weights, axis=0, keepdims=True)).astype(jnp.bfloat16)
    probs_ref[head] = probs
    attended = lax.dot_general(probs, value_ref[:, lanes], TN, preferred_element_type=jnp.float32)
    attended_ref[:, lanes] = attended.astype(jnp.bfloat16)


def scatter_wide(at, links, mine, from_y, via, from_x, result):
    half = result.shape[0] // 2
    quarter = half // 2
    lower, upper = pl.ds(0, half), pl.ds(half, half)
    xp, xm, yy = (at.wide(w) for w in (at.w_xp, at.w_xm, at.w_y))
    ya, yb = from_y
    state = {}

    def add(dx, dy, rows, *others):
        ref = mine(dx, dy).at[rows]
        total = ref[...].astype(jnp.float32)
        for other in others:
            total = total + other[...].astype(jnp.float32)
        return ref, total

    def add_into(dx, dy, rows, *others):
        ref, total = add(dx, dy, rows, *others)
        ref[...] = total.astype(jnp.bfloat16)

    def across(name, slot, dx_dy, start):
        for k, device in ((0, xp), (1, xm)):
            rows = pl.ds(start + k * quarter, quarter)
            state[name, k] = links.put(mine(*dx_dy).at[rows], via.at[slot, k], device)

    def first_a():
        state["ya2"] = links.put(mine(2, 1).at[lower], ya.at[2], yy)
        across("vb1", 1, (2, 1), half)
        across("vb0", 0, (2, 0), half)

    def first_b():
        for dx in (1, 3, 0):
            state["ya%d" % dx] = links.put(mine(dx, 1).at[lower], ya.at[dx], yy)

    def onward(name, slot, dy, start, rows):
        for k, dx, device in ((0, 1, xp), (1, 3, xm)):
            state[name, k].wait_recv()
            add_into(dx, dy, pl.ds(start + k * quarter, quarter), via.at[slot, k])
            state["r" + name, k] = links.put(mine(dx, dy).at[rows], from_x.at[slot, k], device)

    def second():
        state["ya2"].wait_recv()
        add_into(2, 0, lower, ya.at[2])
        across("va", 2, (2, 0), 0)
        onward("vb1", 1, 1, half, upper)
        onward("vb0", 0, 0, half, upper)

    def third():
        for dx in (1, 3):
            state["ya%d" % dx].wait_recv()
            add_into(dx, 0, lower, ya.at[dx])
        onward("va", 2, 0, 0, lower)
        for k in range(2):
            state["rvb1", k].wait_recv()
        add_into(0, 1, upper, from_x.at[1, 0], from_x.at[1, 1])
        state["yb"] = links.put(mine(0, 1).at[upper], yb, yy)

    def fourth():
        state["ya0"].wait_recv()
        for k in range(2):
            state["rva", k].wait_recv()
        result[lower, :] = add(0, 0, lower, ya.at[0], from_x.at[2, 0], from_x.at[2, 1])[1]
        for k in range(2):
            state["rvb0", k].wait_recv()
        state["yb"].wait_recv()
        result[upper, :] = add(0, 0, upper, yb, from_x.at[0, 0], from_x.at[0, 1])[1]

    return first_a, first_b, second, third, fourth


def kernel(
    tile_hbm, target_ref, row_ref, wo_hbm, vw_hbm, query_hbm, key_hbm, value_hbm, position_ref, normed_hbm,
    gin_hbm, gq_ref, gk_ref, gow_ref, gvw_ref, vw_all,
    g_ref, query_ref, key_ref, value_ref, attended_ref, probs, weight, other, out_mine, core_out, core_value,
    ya_out, yb_out, via_out, x_out, ya_val, yb_val, via_val, x_val, gv_own, gv_all,
    hop, hop_target, hop_row, places, landed, landed_places, vw_own,
    relay_send, relay_recv, out_send, out_recv, value_send, value_recv, out_sum_send, out_sum_recv,
    value_sum_send, value_sum_recv, data_send, data_recv, place_send, place_recv, share_send, share_recv,
    core_send, core_recv, gv_send, gv_recv, gin_send, gin_recv, own_sem, tile_sem, local_sem, load_sem,
):
    at = Place()
    loads = [
        pltpu.make_async_copy(src, dst, load_sem.at[k])
        for k, (src, dst) in enumerate(((query_hbm, query_ref), (key_hbm, key_ref), (value_hbm, value_ref)))
    ]
    for load in loads:
        load.start()
    groups = 16
    tok, width = tile_hbm.shape
    chunks, _, cols = hop.shape
    across = (1 - at.s, at.w_y, at.n)
    barrier = greet(
        [across]
        + [at.wide((at.w + i) % groups) for i in range(1, groups)]
        + [(at.s, w, n) for w in (at.w, at.w_core) for n in (at.n_p, at.n_m, at.n_2)]
    )
    landed[:, :, SLOTS:, :] = jnp.zeros((chunks, groups, PAD - SLOTS, cols), landed.dtype)
    pl.semaphore_wait(barrier, 1 + 15 + 6)

    links = Links(relay_send, relay_recv)
    out_links = Links(out_send, out_recv)
    value_links = Links(value_send, value_recv)
    hop_index = [links.put(target_ref, hop_target, across), links.put(row_ref, hop_row, across)]
    hop_data = [links.put(tile_hbm.at[:, pl.ds(k * cols, cols)], hop.at[k], across) for k in range(chunks)]

    half_chunk = vw_hbm.shape[0] // 4

    def share(h, c):
        w, n = at.w - at.core + c, 2 * at.core + h
        src = vw_hbm.at[pl.ds((2 * h + c) * half_chunk, half_chunk)]
        dst = vw_own.at[pl.ds(pl.multiple_of(at.n * half_chunk, half_chunk), half_chunk)]
        mine = (at.core == c) & (at.n == n)
        remote = pltpu.make_async_remote_copy(
            src_ref=src, dst_ref=dst, send_sem=share_send.at[2 * h + c], recv_sem=share_recv.at[at.n],
            device_id=(at.s, w, n), device_id_type=MESH,
        )
        return mine, remote, lambda: pltpu.make_async_copy(src, dst, share_recv.at[at.n]).start()

    out_gather = gather_wide(at, out_links, wo_hbm, weight, local_sem.at[0])
    value_gather = gather_wide(at, value_links, vw_own, vw_all, local_sem.at[1])
    out_gather[0]()
    for h in range(2):
        for c in range(2):
            mine, remote, local = share(h, c)
            pl.when(mine)(local)
            pl.when(jnp.logical_not(mine))(remote.start)

    for copy in hop_index:
        copy.wait_recv()
    target = hop_target[...]
    group = lax.broadcasted_iota(jnp.int32, (groups, tok), 0)
    member = jnp.where(group == target, 1.0, 0.0).astype(jnp.float32)
    before = jnp.where(
        lax.broadcasted_iota(jnp.int32, (tok, tok), 0) < lax.broadcasted_iota(jnp.int32, (tok, tok), 1), 1.0, 0.0
    ).astype(jnp.bfloat16)
    earlier = jnp.dot(member.astype(jnp.bfloat16), before, preferred_element_type=jnp.float32)
    within = jnp.sum(earlier * member, axis=0, keepdims=True).astype(jnp.int32)
    slot = target * PAD + within

    def choose(r):
        return out_mine.at[4 + r // 2, :, pl.ds((r % 2) * tok, tok)]

    for r in range(4):
        wanted = lax.broadcasted_iota(jnp.int32, (256, tok), 0) + r * 256
        choose(r)[...] = jnp.where(wanted == slot, 1.0, 0.0).astype(jnp.bfloat16)

    lane = within + PAD * (at.w % 2)
    to_lane = jnp.where(
        lax.broadcasted_iota(jnp.int32, (128, tok), 0) == lane, 1.0, 0.0
    ).astype(jnp.bfloat16)
    place = hop_row[...] + 1
    high = (place // 32).astype(jnp.float32)
    low = (place % 32).astype(jnp.float32)
    high = lax.dot_general((member * high).astype(jnp.bfloat16), to_lane, NT, preferred_element_type=jnp.float32)
    low = lax.dot_general((member * low).astype(jnp.bfloat16), to_lane, NT, preferred_element_type=jnp.float32)
    lanes = (high * 32.0 + low).astype(jnp.int32)
    places[...] = jnp.broadcast_to(lanes[:, None, :], places.shape)

    def send_place(i):
        t = (at.w + i) % groups
        return pltpu.make_async_remote_copy(
            src_ref=places.at[t], dst_ref=landed_places.at[at.w],
            send_sem=place_send.at[t], recv_sem=place_recv.at[at.w],
            device_id=at.wide(t), device_id_type=MESH,
        )

    def from_packed(k, t):
        rows = pl.ds(pl.multiple_of((t % 4) * PAD, PAD), SLOTS)
        return out_mine.at[t // 4, rows, pl.ds(k * cols, cols)], landed.at[k, at.w, pl.ds(0, SLOTS)]

    def send_rows(k, i):
        t = (at.w + i) % groups
        src, dst = from_packed(k, t)
        return pltpu.make_async_remote_copy(
            src_ref=src, dst_ref=dst, send_sem=data_send.at[k, t], recv_sem=data_recv.at[k, at.w],
            device_id=at.wide(t), device_id_type=MESH,
        )

    pltpu.make_async_copy(places.at[at.w], landed_places.at[at.w], place_recv.at[at.w]).start()

    @pl.loop(1, groups)
    def _(i):
        send_place(i).start()

    def pack(k):
        hop_data[k].wait_recv()
        for r in range(4):
            rows = jnp.dot(choose(r)[...], hop[k], preferred_element_type=jnp.float32)
            out_mine[r, :, pl.ds(k * cols, cols)] = rows.astype(jnp.bfloat16)
        src, dst = from_packed(k, at.w)
        pltpu.make_async_copy(src, dst, data_recv.at[k, at.w]).start()

        @pl.loop(1, groups)
        def _(i):
            send_rows(k, i).start()

    part = tok // 2
    z_p, z_m, on_p, on_m = [], [], [], []

    def unpack(k):
        @pl.loop(0, groups)
        def _(i):
            piece = landed.at[k, i, pl.ds(0, SLOTS)]
            pltpu.make_async_copy(piece, piece, data_recv.at[k, i]).wait()

        rows = landed[k].reshape(groups * PAD, cols)
        for r in range(2):
            placed = jnp.dot(out_mine[6 + r], rows, preferred_element_type=jnp.float32)
            g_ref[at.n, pl.ds(r * part, part), pl.ds(k * cols, cols)] = placed.astype(jnp.bfloat16)
        ref = g_ref.at[at.n, :, pl.ds(k * cols, cols)]
        z_p.append(links.put(ref, ref, at.narrow(at.n_p)))
        z_m.append(links.put(ref, ref, at.narrow(at.n_m)))

    def forward(k):
        z_p[k].wait_recv()
        ref = g_ref.at[at.n_m, pl.ds(0, part), pl.ds(k * cols, cols)]
        on_p.append(links.put(ref, ref, at.narrow(at.n_p)))
        z_m[k].wait_recv()
        ref = g_ref.at[at.n_p, pl.ds(part, part), pl.ds(k * cols, cols)]
        on_m.append(links.put(ref, ref, at.narrow(at.n_m)))

    key_at = lax.broadcasted_iota(jnp.int32, (tok, tok), 0)
    query_at = lax.broadcasted_iota(jnp.int32, (tok, tok), 1)
    earliest = lax.broadcasted_iota(jnp.int32, (1, tok), 1) - position_ref[...]

    def heads(first, last):
        @pl.loop(first, last)
        def _(head):
            allowed = (key_at <= query_at) & (key_at >= earliest)
            attention_forward(head, query_ref, key_ref, value_ref, allowed, probs, attended_ref)

    def wait_places():
        @pl.loop(0, groups)
        def _(i):
            piece = landed_places.at[i]
            pltpu.make_async_copy(piece, piece, place_recv.at[i]).wait()

        arrived = landed_places[...].reshape(groups // 2, 2, 8, 128)
        arrived = (arrived[:, 0] + arrived[:, 1])[:, 0, :]
        for r in range(2):
            token = lax.broadcasted_iota(jnp.int32, (part, 128), 0) + (1 + r * part)
            for k in range(groups // 2):
                here = jnp.where(token == arrived[k : k + 1, :], 1.0, 0.0)
                out_mine[6 + r, :, pl.ds(k * 128, 128)] = here.astype(jnp.bfloat16)

    pack(0)
    for load in loads:
        load.wait()
    heads(0, 2)
    wait_places()
    pack(1)
    out_gather[1]()
    out_gather[2]()
    unpack(0)
    for b in range(4):
        piece = vw_own.at[pl.ds(b * half_chunk, half_chunk)]
        pltpu.make_async_copy(piece, piece, share_recv.at[b]).wait()
    value_gather[0]()
    pack(2)
    unpack(1)
    heads(2, 4)
    pack(3)
    out_gather[3]()
    unpack(2)
    forward(0)
    unpack(3)
    heads(4, 6)
    forward(1)
    value_gather[1]()
    value_gather[2]()
    heads(6, 8)
    out_gather[4]()
    forward(2)

    @pl.loop(1, groups)
    def _(i):
        send_place(i).wait_send()
        for k in range(chunks):
            send_rows(k, i).wait_send()

    out_scatter = Links(out_sum_send, out_sum_recv)
    value_scatter = Links(value_sum_send, value_sum_recv)

    def chip(dx, dy):
        y = at.y if dy == 0 else 1 - at.y
        return ((at.x + dx) % 4) * 2 + y

    def far_first(i):
        return (at.x + 2 + i // 2) % 4, (at.y + 1 + i) % 2

    def as_arriving(i):
        k = i // 2
        return (at.n + k + k // 2 - 2 * (k // 3)) % 4, i % 2

    def terms(which, chip_of, left, right, to_core, mine, landing):
        def send(i):
            x, y = chip_of(i)
            return pltpu.make_async_remote_copy(
                src_ref=to_core(x, y), dst_ref=landing.at[x * 2 + y],
                send_sem=core_send.at[which, i], recv_sem=core_recv.at[which, i],
                device_id=at.wide(at.w_core), device_id_type=MESH,
            )

        def theirs(first, last):
            @pl.loop(first, last)
            def _(i):
                x, y = chip_of(i)
                term = lax.dot_general(left(x, y, 1 - at.core), right[...], TN, preferred_element_type=jnp.float32)
                to_core(x, y)[...] = term.astype(jnp.bfloat16)
                send(i).start()

        def ours(first, last):
            @pl.loop(first, last)
            def _(i):
                x, y = chip_of(i)
                term = lax.dot_general(left(x, y, at.core), right[...], TN, preferred_element_type=jnp.float32)
                send(i).wait_recv()
                term = term + landing[x * 2 + y].astype(jnp.float32)
                mine(x * 2 + y)[...] = term.astype(jnp.bfloat16)

        def drain():
            @pl.loop(0, 8)
            def _(i):
                send(i).wait_send()

        return theirs, ours, drain

    def g_columns(x, y, core):
        return g_ref[x, :, pl.ds(pl.multiple_of(y * 512 + core * 256, 256), 256)]

    def normed_columns(x, y, core):
        return other[:, pl.ds(pl.multiple_of(x * 1024 + y * 512 + core * 256, 256), 256)]

    def in_other(x, y):
        return other.at[pl.ds(pl.multiple_of(y * 256, 256), 256), pl.ds(pl.multiple_of(x * 1024, 1024), 1024)]

    theirs, ours, drain_core = terms(0, as_arriving, g_columns, attended_ref, in_other, lambda j: out_mine.at[j], core_out)
    out_steps = scatter_wide(
        at, out_scatter, lambda dx, dy: out_mine.at[chip(dx, dy)], (ya_out, yb_out), via_out, x_out, gow_ref
    )
    theirs(0, 2)
    forward(3)
    theirs(2, 6)
    ours(0, 6)
    value_gather[3]()
    for k in range(chunks):
        on_p[k].wait_recv()
        on_m[k].wait_recv()
    theirs(6, 8)
    ours(6, 8)
    out_steps[0]()
    out_steps[1]()
    drain_core()
    load_normed = pltpu.make_async_copy(normed_hbm, other, local_sem.at[2])
    load_normed.start()
    out_gather[5]()

    scale = HEAD_DIM**-0.5

    def gv_copies(pair):
        def copy(k, src, device):
            return pltpu.make_async_remote_copy(
                src_ref=src, dst_ref=src, send_sem=gv_send.at[k, pair], recv_sem=gv_recv.at[k, pair],
                device_id=at.narrow(device), device_id_type=MESH,
            )

        mine = gv_all.at[at.n, pair]
        on_p = gv_all.at[at.n_m, pair, pl.ds(0, part)]
        on_m = gv_all.at[at.n_p, pair, pl.ds(part, part)]
        return copy(0, mine, at.n_p), copy(1, mine, at.n_m), copy(2, on_p, at.n_p), copy(3, on_m, at.n_m)

    def forward_gv(pair):
        to_p, to_m, on_p, on_m = gv_copies(pair)
        to_p.wait_recv()
        on_p.start()
        to_m.wait_recv()
        on_m.start()

    def attend(pair):
        lanes = pl.ds(pair * 256, 256)
        total = jnp.zeros((tok, 256), jnp.float32)
        for b in range(4):
            block = weight[4 * b : 4 * b + 4, :, lanes].reshape(width, 256)
            total = total + jnp.dot(g_ref[b], block, preferred_element_type=jnp.float32)
        both = total.astype(jnp.bfloat16)
        for h in range(2):
            cols = pl.ds(pair * 256 + h * HEAD_DIM, HEAD_DIM)
            gout = both[:, h * HEAD_DIM : (h + 1) * HEAD_DIM]
            prob = probs[2 * pair + h]
            dprob = lax.dot_general(value_ref[:, cols], gout, NT, preferred_element_type=jnp.float32)
            wide_prob = prob.astype(jnp.float32)
            delta = jnp.sum(wide_prob * dprob, axis=0, keepdims=True)
            dscore = (wide_prob * (dprob - delta)).astype(jnp.bfloat16)
            gv = jnp.dot(prob, gout, preferred_element_type=jnp.float32).astype(jnp.bfloat16)
            gv_own[:, cols] = gv
            gv_all[at.n, pair, :, pl.ds(h * HEAD_DIM, HEAD_DIM)] = gv
            gk = jnp.dot(dscore, query_ref[:, cols], preferred_element_type=jnp.float32) * scale
            gk_ref[:, cols] = gk.astype(jnp.bfloat16)
            gq = lax.dot_general(dscore, key_ref[:, cols], TN, preferred_element_type=jnp.float32) * scale
            gq_ref[:, cols] = gq.astype(jnp.bfloat16)
        to_p, to_m, _, _ = gv_copies(pair)
        to_p.start()
        to_m.start()
        if pair > 0:
            forward_gv(pair - 1)

    attend(0)
    attend(1)
    value_gather[4]()
    attend(2)
    out_steps[2]()
    attend(3)
    out_steps[3]()
    out_links.drain()

    def load_tile(tile):
        return pltpu.make_async_copy(vw_all.at[pl.ds(4 * tile, 4)], core_out.at[pl.ds(4 * (tile % 2), 4)], tile_sem.at[tile % 2])

    load_normed.wait()
    theirs, ours, drain_value = terms(
        1, far_first, normed_columns, gv_own, lambda x, y: weight.at[x * 2 + y], lambda j: weight.at[8 + j], core_value
    )
    value_steps = scatter_wide(
        at, value_scatter, lambda dx, dy: weight.at[8 + chip(dx, dy)], (ya_val, yb_val), via_val, x_val, gvw_ref
    )
    theirs(0, 8)
    forward_gv(3)
    ours(0, 2)
    value_steps[0]()
    ours(2, 8)
    value_steps[1]()
    value_gather[5]()
    load_tile(0).start()
    load_tile(1).start()
    for pair in range(4):
        _, _, on_p, on_m = gv_copies(pair)
        on_p.wait_recv()
        on_m.wait_recv()

    def gin_copies(tile, y):
        def copy(k, src, dst, device):
            return pltpu.make_async_remote_copy(
                src_ref=src, dst_ref=dst, send_sem=gin_send.at[k, 2 * tile + y], recv_sem=gin_recv.at[k, 2 * tile + y],
                device_id=at.narrow(device), device_id_type=MESH,
            )

        def chunk(n, start, size):
            cols = pl.ds(pl.multiple_of(tile * 1024 + y * 512 + n * 128, 128), 128)
            return gin_hbm.at[pl.ds(start, size), cols]

        src, dst = hop.at[tile, :, pl.ds(y * 128, 128)], chunk(at.n, 0, tok)
        on_p, on_m = chunk(at.n_m, 0, part), chunk(at.n_p, part, part)
        own = pltpu.make_async_copy(src, dst, own_sem.at[2 * tile + y])
        return copy(0, src, dst, at.n_p), copy(1, src, dst, at.n_m), copy(2, on_p, on_p, at.n_p), copy(3, on_m, on_m, at.n_m), own

    def forward_gin(tile):
        for y in range(2):
            to_p, to_m, on_p, on_m, _ = gin_copies(tile, y)
            to_p.wait_recv()
            on_p.start()
            to_m.wait_recv()
            on_m.start()

    for tile in range(4):
        load_tile(tile).wait()
        chunk = pl.multiple_of(at.n * 128, 128)
        low = g_ref[tile, :, pl.ds(chunk, 128)]
        high = g_ref[tile, :, pl.ds(pl.multiple_of(chunk + 512, 128), 128)]
        total = jnp.concatenate([low, high], axis=1).astype(jnp.float32)
        for z in range(4):
            for pair in range(4):
                block = core_out[
                    4 * (tile % 2) : 4 * (tile % 2) + 4, z * 64 : (z + 1) * 64, pair * 256 : (pair + 1) * 256
                ].reshape(256, 256)
                total = total + lax.dot_general(gv_all[z, pair], block, NT, preferred_element_type=jnp.float32)
        hop[tile] = total.astype(jnp.bfloat16)
        for y in range(2):
            to_p, to_m, _, _, own = gin_copies(tile, y)
            to_p.start()
            to_m.start()
            own.start()
        if tile < 2:
            load_tile(tile + 2).start()

    out_steps[4]()
    forward_gin(0)
    value_steps[2]()
    forward_gin(1)
    forward_gin(2)
    value_steps[3]()
    forward_gin(3)
    value_steps[4]()
    drain_value()
    for tile in range(4):
        for y in range(2):
            to_p, to_m, on_p, on_m, own = gin_copies(tile, y)
            on_p.wait_recv()
            on_m.wait_recv()
            own.wait()
            for copy in (to_p, to_m, on_p, on_m):
                copy.wait_send()
        for copy in gv_copies(tile):
            copy.wait_send()
    for h in range(2):
        for c in range(2):
            mine, remote, local = share(h, c)
            pl.when(jnp.logical_not(mine))(remote.wait_send)

    for used in (links, value_links, out_scatter, value_scatter):
        used.drain()


def backward(tile, target, row, wo, vw, query, key, value, position, normed):
    tok, width = tile.shape
    rows = wo.shape[0]
    half = rows // 2
    chunks = 4
    bf16, f32, i32 = jnp.bfloat16, jnp.float32, jnp.int32
    dma = pltpu.SemaphoreType.DMA
    vmem = pl.BlockSpec(memory_space=pltpu.VMEM)
    hbm = pl.BlockSpec(memory_space=pl.ANY)

    def buffer(*shape):
        return pltpu.VMEM(shape, bf16)

    landing = [
        buffer(4, half, width),
        buffer(half, width),
        buffer(3, 2, half // 2, width),
        buffer(3, 2, half, width),
    ]
    return pl.pallas_call(
        kernel,
        out_shape=(
            jax.ShapeDtypeStruct((tok, 4 * width), bf16),
            jax.ShapeDtypeStruct((tok, width), bf16),
            jax.ShapeDtypeStruct((tok, width), bf16),
            jax.ShapeDtypeStruct((rows, width), f32),
            jax.ShapeDtypeStruct((rows, width), f32),
            jax.ShapeDtypeStruct((16, rows, width), bf16),
        ),
        in_specs=[hbm, vmem, vmem, hbm, hbm, hbm, hbm, hbm, vmem, hbm],
        out_specs=(hbm, vmem, vmem, vmem, vmem, hbm),
        scratch_shapes=[
            buffer(4, tok, width),
            *[buffer(tok, width)] * 4,
            buffer(width // HEAD_DIM, tok, tok),
            buffer(16, rows, width),
            buffer(tok, 4 * width),
            *[buffer(8, rows, width)] * 3,
            *landing,
            *landing,
            buffer(tok, width),
            buffer(4, 4, tok, 256),
            buffer(chunks, tok, width // chunks),
            pltpu.VMEM(target.shape, i32),
            pltpu.VMEM(row.shape, i32),
            pltpu.VMEM((16, 8, 128), i32),
            buffer(chunks, 16, PAD, width // chunks),
            pltpu.VMEM((16, 8, 128), i32),
            buffer(rows, width),
            *[dma((22,))] * 2,
            *[dma((20,))] * 4,
            *[dma((17,))] * 4,
            *[dma((chunks, 16))] * 2,
            *[dma((16,))] * 2,
            *[dma((4,))] * 2,
            *[dma((2, 8))] * 2,
            *[dma((4, 4))] * 2,
            *[dma((4, 8))] * 2,
            dma((8,)), dma((2,)), dma((3,)), dma((3,)),
        ],
        compiler_params=pltpu.CompilerParams(
            collective_id=0, has_side_effects=True, vmem_limit_bytes=63 * 1024 * 1024
        ),
        name="relay_backward_and_sum",
    )(tile, target, row, wo, vw, query, key, value, position, normed)


def shards(boundary_grad, tile_target, tile_row, normed_input, query, keys, values, positions, out_weight, value_weight):
    outputs = backward(
        boundary_grad[0], tile_target, tile_row, out_weight[0], value_weight[0], query[0], keys[0], values[0], positions,
        normed_input[0],
    )
    return tuple(output[None] for output in outputs[:5])


def solution(mesh):
    split = P("section", "wide", "narrow")
    rows = P("section", "wide")
    in_specs = (split, rows, rows, P("section", "wide", None), split, split, split, rows, split, split)
    out_specs = (P("section", "wide", None), split, split, split, split)
    return jax.shard_map(shards, mesh=mesh, in_specs=in_specs, out_specs=out_specs, check_vma=False)
```

time: 227 us -> 185 us (0.81)
  Pallas kernels: 215 us -> 171 us
    pallas_call x2 -> x1, Pallas kernels: 215 us -> 171 us  [backward(): pl.pallas_call(kernel, out_shape=(jax.ShapeDtypeStruct((tok, 4 * width),...]
where the time goes in v3:
time: 185 us; the launch traced here: 181 us
  Pallas kernels  171 us (92%)
  local copies, waits for them, and re-layouts  8.74 us (5%)
    pallas_call x1, Pallas kernels, backward(): pl.pallas_call(kernel, out_shape=(jax.ShapeDtypeStruct((tok, 4 * width),...  171 us
    unnamed x13, local copies, waits for them, and re-layouts  8.74 us

profile of v3, /device:TPU:27, one launch (start us, length us, event | category | flops | bytes accessed | tf_op | source)
XLA Modules:
  0.0 180.8 jit_solution(5116046035864211365)
XLA Ops:
  0.6 171.4 %relay_backward_and_sum.1 = (bf16[512,4096]{1,0:T(8,128)(2,1)}, bf16[512,1024]{1,0:T(8,128)(2,1)}, bf16[512,1024]{1,0:T(8,128)(2,1)}, f32[256,1024]{1,0:T(8,128)...) custom-call(bf16[512,1024]{1,0:T(8,128)(2,1)} %bitcast.14, s32[1,512]{1,0:T(1,128)} %target_ref.1, ...), custom_call_target="tpu_custom_call" | custom-call | tf_op jit(solution)/shard_map/relay_backward_and_sum/pallas_call | solution.py:680
  172.1 0.0 copy-start.3
  172.1 0.0 copy-start.2
  172.1 4.8 %copy.20 = bf16[1,512,4096]{2,1,0:T(8,128)(2,1)} copy(bf16[1,512,4096]{2,1,0:T(8,128)(2,1)} %bitcast.13) | data formatting | bytes 8388608
  176.9 0.0 copy-done.3
  176.9 0.0 copy-start.1
  176.9 0.0 copy-start
  177.0 1.0 copy.21
  177.9 0.0 copy-done.2
  177.9 1.0 copy.22
  178.9 0.0 copy-done.1
  178.9 1.0 copy.23
  179.9 0.0 copy-done
  179.9 1.0 copy.24
Async XLA Ops:
  172.1 4.9 %copy-start.3 = (bf16[512,1024]{1,0:T(8,128)(2,1)S(1)}, bf16[512,1024]{1,0:T(8,128)(2,1)}, u32[]{:S(2)}) copy-start(bf16[512,1024]{1,0:T(8,128)(2,1)} %get-tuple-element.11) | copy-start | bytes 3145732
  172.1 5.8 %copy-start.2 = (bf16[512,1024]{1,0:T(8,128)(2,1)S(1)}, bf16[512,1024]{1,0:T(8,128)(2,1)}, u32[]{:S(2)}) copy-start(bf16[512,1024]{1,0:T(8,128)(2,1)} %get-tuple-element.12) | copy-start | bytes 3145732
  176.9 1.9 %copy-start.1 = (f32[256,1024]{1,0:T(8,128)S(1)}, f32[256,1024]{1,0:T(8,128)}, u32[]{:S(2)}) copy-start(f32[256,1024]{1,0:T(8,128)} %get-tuple-element.13) | copy-start | bytes 3145732
  176.9 2.9 %copy-start = (f32[256,1024]{1,0:T(8,128)S(1)}, f32[256,1024]{1,0:T(8,128)}, u32[]{:S(2)}) copy-start(f32[256,1024]{1,0:T(8,128)} %get-tuple-element.14) | copy-start | bytes 3145732

commit v4 on v3

--- a/solution.py
+++ b/solution.py
@@ -72,10 +72,17 @@
     return barrier
 
 
+def split_rows(rows):
+    low = rows * 7 // 16
+    return low, low + rows // 4
+
+
 def gather_wide(at, links, own, full, local_sem):
-    half = own.shape[0] // 2
-    lower, upper = pl.ds(0, half), pl.ds(half, half)
-    third, fourth = pl.ds(half, half // 2), pl.ds(half + half // 2, half // 2)
+    rows = own.shape[0]
+    low, middle = split_rows(rows)
+    lower, upper = pl.ds(0, low), pl.ds(low, rows - low)
+    third, fourth = pl.ds(low, middle - low), pl.ds(middle, rows - middle)
+    one, two = pl.ds(0, rows // 2), pl.ds(rows // 2, rows // 2)
     xp, xm, yy, cc = (at.wide(w) for w in (at.w_xp, at.w_xm, at.w_y, at.w_core))
 
     def send(w, device, rows=None):
@@ -100,11 +107,11 @@
 
     def second_x():
         state["xp"].wait_recv()
-        state["f_p"] = send(at.w_xm, xp, lower)
+        state["f_p"] = send(at.w_xm, xp, one)
         state["g_m"] = send(at.w_xm, yy, lower)
         state["c_m"] = send(at.w_xm, cc)
         state["xm"].wait_recv()
-        state["f_m"] = send(at.w_xp, xm, upper)
+        state["f_m"] = send(at.w_xp, xm, two)
         state["g_p"] = send(at.w_xp, yy, lower)
         state["c_p"] = send(at.w_xp, cc)
 
@@ -148,9 +155,11 @@
 
 
 def scatter_wide(at, links, mine, from_y, via, from_x, result):
-    half = result.shape[0] // 2
-    quarter = half // 2
-    lower, upper = pl.ds(0, half), pl.ds(half, half)
+    rows = result.shape[0]
+    low, middle = split_rows(rows)
+    lower, upper = pl.ds(0, low), pl.ds(low, rows - low)
+    low_parts = pl.ds(0, rows // 4), pl.ds(rows // 4, low - rows // 4)
+    high_parts = pl.ds(low, middle - low), pl.ds(middle, rows - middle)
     xp, xm, yy = (at.wide(w) for w in (at.w_xp, at.w_xm, at.w_y))
     ya, yb = from_y
     state = {}
@@ -166,65 +175,71 @@
         ref, total = add(dx, dy, rows, *others)
         ref[...] = total.astype(jnp.bfloat16)
 
-    def across(name, slot, dx_dy, start):
+    def across(name, slot, dx_dy, parts):
         for k, device in ((0, xp), (1, xm)):
-            rows = pl.ds(start + k * quarter, quarter)
-            state[name, k] = links.put(mine(*dx_dy).at[rows], via.at[slot, k], device)
+            landing = via.at[slot, k, pl.ds(0, parts[k].size)]
+            state[name, k] = links.put(mine(*dx_dy).at[parts[k]], landing, device)
 
     def first_a():
         state["ya2"] = links.put(mine(2, 1).at[lower], ya.at[2], yy)
-        across("vb1", 1, (2, 1), half)
-        across("vb0", 0, (2, 0), half)
+        across("vb1", 1, (2, 1), high_parts)
+        across("vb0", 0, (2, 0), high_parts)
 
     def first_b():
         for dx in (1, 3, 0):
             state["ya%d" % dx] = links.put(mine(dx, 1).at[lower], ya.at[dx], yy)
 
-    def onward(name, slot, dy, start, rows):
+    def onward(name, slot, dy, parts, rows):
         for k, dx, device in ((0, 1, xp), (1, 3, xm)):
             state[name, k].wait_recv()
-            add_into(dx, dy, pl.ds(start + k * quarter, quarter), via.at[slot, k])
-            state["r" + name, k] = links.put(mine(dx, dy).at[rows], from_x.at[slot, k], device)
+            add_into(dx, dy, parts[k], via.at[slot, k, pl.ds(0, parts[k].size)])
+            landing = from_x.at[slot, k, pl.ds(0, rows.size)]
+            state["r" + name, k] = links.put(mine(dx, dy).at[rows], landing, device)
 
     def second():
         state["ya2"].wait_recv()
         add_into(2, 0, lower, ya.at[2])
-        across("va", 2, (2, 0), 0)
-        onward("vb1", 1, 1, half, upper)
-        onward("vb0", 0, 0, half, upper)
+        across("va", 2, (2, 0), low_parts)
+        onward("vb1", 1, 1, high_parts, upper)
+        onward("vb0", 0, 0, high_parts, upper)
+
+    def upper_from_x(slot):
+        return [from_x.at[slot, k] for k in range(2)]
 
     def third():
         for dx in (1, 3):
             state["ya%d" % dx].wait_recv()
             add_into(dx, 0, lower, ya.at[dx])
-        onward("va", 2, 0, 0, lower)
+        onward("va", 2, 0, low_parts, lower)
         for k in range(2):
             state["rvb1", k].wait_recv()
-        add_into(0, 1, upper, from_x.at[1, 0], from_x.at[1, 1])
+        add_into(0, 1, upper, *upper_from_x(1))
         state["yb"] = links.put(mine(0, 1).at[upper], yb, yy)
 
     def fourth():
         state["ya0"].wait_recv()
         for k in range(2):
             state["rva", k].wait_recv()
-        result[lower, :] = add(0, 0, lower, ya.at[0], from_x.at[2, 0], from_x.at[2, 1])[1]
+        lower_from_x = [from_x.at[2, k, pl.ds(0, low)] for k in range(2)]
+        result[lower, :] = add(0, 0, lower, ya.at[0], *lower_from_x)[1]
         for k in range(2):
             state["rvb0", k].wait_recv()
         state["yb"].wait_recv()
-        result[upper, :] = add(0, 0, upper, yb, from_x.at[0, 0], from_x.at[0, 1])[1]
+        result[upper, :] = add(0, 0, upper, yb, *upper_from_x(0))[1]
 
     return first_a, first_b, second, third, fourth
 
 
 def kernel(
     tile_hbm, target_ref, row_ref, wo_hbm, vw_hbm, query_hbm, key_hbm, value_hbm, position_ref, normed_hbm,
-    gin_hbm, gq_ref, gk_ref, gow_ref, gvw_ref, vw_all,
+    gin_hbm, gq_hbm, gk_hbm, gow_hbm, gvw_hbm, vw_all,
+    gq_ref, gk_ref, gow_ref, gvw_ref,
     g_ref, query_ref, key_ref, value_ref, attended_ref, probs, weight, other, out_mine, core_out, core_value,
     ya_out, yb_out, via_out, x_out, ya_val, yb_val, via_val, x_val, gv_own, gv_all,
-    hop, hop_target, hop_row, places, landed, landed_places, vw_own,
+    hop, hop_slot, hop_places, slots, places, landed, landed_places, vw_own,
     relay_send, relay_recv, out_send, out_recv, value_send, value_recv, out_sum_send, out_sum_recv,
     value_sum_send, value_sum_recv, data_send, data_recv, place_send, place_recv, share_send, share_recv,
-    core_send, core_recv, gv_send, gv_recv, gin_send, gin_recv, own_sem, tile_sem, local_sem, load_sem,
+    core_send, core_recv, gv_send, gv_recv, gin_send, gin_recv, own_sem, tile_sem, local_sem, load_sem, store_sem,
 ):
     at = Place()
     loads = [
@@ -242,13 +257,33 @@
         + [at.wide((at.w + i) % groups) for i in range(1, groups)]
         + [(at.s, w, n) for w in (at.w, at.w_core) for n in (at.n_p, at.n_m, at.n_2)]
     )
+    target = target_ref[...]
+    group = lax.broadcasted_iota(jnp.int32, (groups, tok), 0)
+    member = jnp.where(group == target, 1.0, 0.0).astype(jnp.float32)
+    before = jnp.where(
+        lax.broadcasted_iota(jnp.int32, (tok, tok), 0) < lax.broadcasted_iota(jnp.int32, (tok, tok), 1), 1.0, 0.0
+    ).astype(jnp.bfloat16)
+    earlier = jnp.dot(member.astype(jnp.bfloat16), before, preferred_element_type=jnp.float32)
+    within = jnp.sum(earlier * member, axis=0, keepdims=True).astype(jnp.int32)
+    slots[...] = jnp.broadcast_to(target * PAD + within, slots.shape)
+    lane = within + PAD * (at.w % 2)
+    to_lane = jnp.where(
+        lax.broadcasted_iota(jnp.int32, (128, tok), 0) == lane, 1.0, 0.0
+    ).astype(jnp.bfloat16)
+    place = row_ref[...] + 1
+    high = (place // 32).astype(jnp.float32)
+    low = (place % 32).astype(jnp.float32)
+    high = lax.dot_general((member * high).astype(jnp.bfloat16), to_lane, NT, preferred_element_type=jnp.float32)
+    low = lax.dot_general((member * low).astype(jnp.bfloat16), to_lane, NT, preferred_element_type=jnp.float32)
+    lanes = (high * 32.0 + low).astype(jnp.int32)
+    places[...] = jnp.broadcast_to(lanes[:, None, :], places.shape)
     landed[:, :, SLOTS:, :] = jnp.zeros((chunks, groups, PAD - SLOTS, cols), landed.dtype)
     pl.semaphore_wait(barrier, 1 + 15 + 6)
 
     links = Links(relay_send, relay_recv)
     out_links = Links(out_send, out_recv)
     value_links = Links(value_send, value_recv)
-    hop_index = [links.put(target_ref, hop_target, across), links.put(row_ref, hop_row, across)]
+    hop_index = [links.put(slots, hop_slot, across), links.put(places, hop_places, across)]
     hop_data = [links.put(tile_hbm.at[:, pl.ds(k * cols, cols)], hop.at[k], across) for k in range(chunks)]
 
     half_chunk = vw_hbm.shape[0] // 4
@@ -273,17 +308,8 @@
             pl.when(mine)(local)
             pl.when(jnp.logical_not(mine))(remote.start)
 
-    for copy in hop_index:
-        copy.wait_recv()
-    target = hop_target[...]
-    group = lax.broadcasted_iota(jnp.int32, (groups, tok), 0)
-    member = jnp.where(group == target, 1.0, 0.0).astype(jnp.float32)
-    before = jnp.where(
-        lax.broadcasted_iota(jnp.int32, (tok, tok), 0) < lax.broadcasted_iota(jnp.int32, (tok, tok), 1), 1.0, 0.0
-    ).astype(jnp.bfloat16)
-    earlier = jnp.dot(member.astype(jnp.bfloat16), before, preferred_element_type=jnp.float32)
-    within = jnp.sum(earlier * member, axis=0, keepdims=True).astype(jnp.int32)
-    slot = target * PAD + within
+    hop_index[0].wait_recv()
+    slot = hop_slot[0:1, :]
 
     def choose(r):
         return out_mine.at[4 + r // 2, :, pl.ds((r % 2) * tok, tok)]
@@ -292,22 +318,12 @@
         wanted = lax.broadcasted_iota(jnp.int32, (256, tok), 0) + r * 256
         choose(r)[...] = jnp.where(wanted == slot, 1.0, 0.0).astype(jnp.bfloat16)
 
-    lane = within + PAD * (at.w % 2)
-    to_lane = jnp.where(
-        lax.broadcasted_iota(jnp.int32, (128, tok), 0) == lane, 1.0, 0.0
-    ).astype(jnp.bfloat16)
-    place = hop_row[...] + 1
-    high = (place // 32).astype(jnp.float32)
-    low = (place % 32).astype(jnp.float32)
-    high = lax.dot_general((member * high).astype(jnp.bfloat16), to_lane, NT, preferred_element_type=jnp.float32)
-    low = lax.dot_general((member * low).astype(jnp.bfloat16), to_lane, NT, preferred_element_type=jnp.float32)
-    lanes = (high * 32.0 + low).astype(jnp.int32)
-    places[...] = jnp.broadcast_to(lanes[:, None, :], places.shape)
+    hop_index[1].wait_recv()
 
     def send_place(i):
         t = (at.w + i) % groups
         return pltpu.make_async_remote_copy(
-            src_ref=places.at[t], dst_ref=landed_places.at[at.w],
+            src_ref=hop_places.at[t], dst_ref=landed_places.at[at.w],
             send_sem=place_send.at[t], recv_sem=place_recv.at[at.w],
             device_id=at.wide(t), device_id_type=MESH,
         )
@@ -324,7 +340,7 @@
             device_id=at.wide(t), device_id_type=MESH,
         )
 
-    pltpu.make_async_copy(places.at[at.w], landed_places.at[at.w], place_recv.at[at.w]).start()
+    pltpu.make_async_copy(hop_places.at[at.w], landed_places.at[at.w], place_recv.at[at.w]).start()
 
     @pl.loop(1, groups)
     def _(i):
@@ -391,40 +407,26 @@
                 here = jnp.where(token == arrived[k : k + 1, :], 1.0, 0.0)
                 out_mine[6 + r, :, pl.ds(k * 128, 128)] = here.astype(jnp.bfloat16)
 
-    pack(0)
-    for load in loads:
-        load.wait()
-    heads(0, 2)
-    wait_places()
-    pack(1)
-    out_gather[1]()
-    out_gather[2]()
-    unpack(0)
-    for b in range(4):
-        piece = vw_own.at[pl.ds(b * half_chunk, half_chunk)]
-        pltpu.make_async_copy(piece, piece, share_recv.at[b]).wait()
-    value_gather[0]()
-    pack(2)
-    unpack(1)
-    heads(2, 4)
-    pack(3)
-    out_gather[3]()
-    unpack(2)
-    forward(0)
-    unpack(3)
-    heads(4, 6)
-    forward(1)
-    value_gather[1]()
-    value_gather[2]()
-    heads(6, 8)
-    out_gather[4]()
-    forward(2)
-
-    @pl.loop(1, groups)
-    def _(i):
-        send_place(i).wait_send()
+    def wait_loads():
+        for load in loads:
+            load.wait()
+
+    def wait_share():
+        for b in range(4):
+            piece = vw_own.at[pl.ds(b * half_chunk, half_chunk)]
+            pltpu.make_async_copy(piece, piece, share_recv.at[b]).wait()
+
+    def drain_rows():
+        @pl.loop(1, groups)
+        def _(i):
+            send_place(i).wait_send()
+            for k in range(chunks):
+                send_rows(k, i).wait_send()
+
+    def wait_gathered():
         for k in range(chunks):
-            send_rows(k, i).wait_send()
+            on_p[k].wait_recv()
+            on_m[k].wait_recv()
 
     out_scatter = Links(out_sum_send, out_sum_recv)
     value_scatter = Links(value_sum_send, value_sum_recv)
@@ -482,26 +484,11 @@
     def in_other(x, y):
         return other.at[pl.ds(pl.multiple_of(y * 256, 256), 256), pl.ds(pl.multiple_of(x * 1024, 1024), 1024)]
 
-    theirs, ours, drain_core = terms(0, as_arriving, g_columns, attended_ref, in_other, lambda j: out_mine.at[j], core_out)
+    theirs_out, ours_out, drain_core = terms(0, as_arriving, g_columns, attended_ref, in_other, lambda j: out_mine.at[j], core_out)
     out_steps = scatter_wide(
         at, out_scatter, lambda dx, dy: out_mine.at[chip(dx, dy)], (ya_out, yb_out), via_out, x_out, gow_ref
     )
-    theirs(0, 2)
-    forward(3)
-    theirs(2, 6)
-    ours(0, 6)
-    value_gather[3]()
-    for k in range(chunks):
-        on_p[k].wait_recv()
-        on_m[k].wait_recv()
-    theirs(6, 8)
-    ours(6, 8)
-    out_steps[0]()
-    out_steps[1]()
-    drain_core()
     load_normed = pltpu.make_async_copy(normed_hbm, other, local_sem.at[2])
-    load_normed.start()
-    out_gather[5]()
 
     scale = HEAD_DIM**-0.5
 
@@ -549,41 +536,21 @@
         to_p, to_m, _, _ = gv_copies(pair)
         to_p.start()
         to_m.start()
-        if pair > 0:
-            forward_gv(pair - 1)
-
-    attend(0)
-    attend(1)
-    value_gather[4]()
-    attend(2)
-    out_steps[2]()
-    attend(3)
-    out_steps[3]()
-    out_links.drain()
 
     def load_tile(tile):
         return pltpu.make_async_copy(vw_all.at[pl.ds(4 * tile, 4)], core_out.at[pl.ds(4 * (tile % 2), 4)], tile_sem.at[tile % 2])
 
-    load_normed.wait()
-    theirs, ours, drain_value = terms(
+    theirs_value, ours_value, drain_value = terms(
         1, far_first, normed_columns, gv_own, lambda x, y: weight.at[x * 2 + y], lambda j: weight.at[8 + j], core_value
     )
     value_steps = scatter_wide(
         at, value_scatter, lambda dx, dy: weight.at[8 + chip(dx, dy)], (ya_val, yb_val), via_val, x_val, gvw_ref
     )
-    theirs(0, 8)
-    forward_gv(3)
-    ours(0, 2)
-    value_steps[0]()
-    ours(2, 8)
-    value_steps[1]()
-    value_gather[5]()
-    load_tile(0).start()
-    load_tile(1).start()
-    for pair in range(4):
-        _, _, on_p, on_m = gv_copies(pair)
-        on_p.wait_recv()
-        on_m.wait_recv()
+    def wait_gv():
+        for pair in range(4):
+            _, _, on_p, on_m = gv_copies(pair)
+            on_p.wait_recv()
+            on_m.wait_recv()
 
     def gin_copies(tile, y):
         def copy(k, src, dst, device):
@@ -609,7 +576,7 @@
             to_m.wait_recv()
             on_m.start()
 
-    for tile in range(4):
+    def gin(tile):
         load_tile(tile).wait()
         chunk = pl.multiple_of(at.n * 128, 128)
         low = g_ref[tile, :, pl.ds(chunk, 128)]
@@ -630,14 +597,92 @@
         if tile < 2:
             load_tile(tile + 2).start()
 
-    out_steps[4]()
+    out_first, out_second_y, out_second_x, out_third, out_fourth, out_last = out_gather
+    value_first, value_second_y, value_second_x, value_third, value_fourth, value_last = value_gather
+    out_sum_a, out_sum_b, out_sum_second, out_sum_third, out_sum_fourth = out_steps
+    value_sum_a, value_sum_b, value_sum_second, value_sum_third, value_sum_fourth = value_steps
+
+    stores = [
+        pltpu.make_async_copy(src, dst, store_sem.at[k])
+        for k, (src, dst) in enumerate(((gq_ref, gq_hbm), (gk_ref, gk_hbm), (gow_ref, gow_hbm), (gvw_ref, gvw_hbm)))
+    ]
+
+    wait_loads()
+    heads(0, 2)
+    pack(0)
+    wait_places()
+    pack(1)
+    unpack(0)
+    out_second_y()
+    out_second_x()
+    pack(2)
+    unpack(1)
+    heads(2, 4)
+    out_third()
+    pack(3)
+    wait_share()
+    value_first()
+    unpack(2)
+    forward(0)
+    unpack(3)
+    out_fourth()
+    forward(1)
+    heads(4, 8)
+    value_second_y()
+    value_second_x()
+    forward(2)
+    drain_rows()
+    theirs_out(0, 2)
+    forward(3)
+    theirs_out(2, 6)
+    ours_out(0, 6)
+    value_third()
+    wait_gathered()
+    out_last()
+    attend(0)
+    theirs_out(6, 8)
+    ours_out(6, 8)
+    out_sum_a()
+    out_sum_b()
+    drain_core()
+    load_normed.start()
+    attend(1)
+    forward_gv(0)
+    value_fourth()
+    attend(2)
+    forward_gv(1)
+    out_sum_second()
+    attend(3)
+    stores[0].start()
+    stores[1].start()
+    forward_gv(2)
+    out_sum_third()
+    out_links.drain()
+    load_normed.wait()
+    theirs_value(0, 8)
+    forward_gv(3)
+    ours_value(0, 2)
+    value_sum_a()
+    ours_value(2, 8)
+    value_sum_b()
+    value_last()
+    load_tile(0).start()
+    load_tile(1).start()
+    wait_gv()
+    gin(0)
+    gin(1)
+    gin(2)
+    gin(3)
+    out_sum_fourth()
+    stores[2].start()
     forward_gin(0)
-    value_steps[2]()
+    value_sum_second()
     forward_gin(1)
     forward_gin(2)
-    value_steps[3]()
+    value_sum_third()
     forward_gin(3)
-    value_steps[4]()
+    value_sum_fourth()
+    stores[3].start()
     drain_value()
     for tile in range(4):
         for y in range(2):
@@ -656,12 +701,14 @@
 
     for used in (links, value_links, out_scatter, value_scatter):
         used.drain()
+    for store in stores:
+        store.wait()
 
 
 def backward(tile, target, row, wo, vw, query, key, value, position, normed):
     tok, width = tile.shape
     rows = wo.shape[0]
-    half = rows // 2
+    low, middle = split_rows(rows)
     chunks = 4
     bf16, f32, i32 = jnp.bfloat16, jnp.float32, jnp.int32
     dma = pltpu.SemaphoreType.DMA
@@ -672,10 +719,10 @@
         return pltpu.VMEM(shape, bf16)
 
     landing = [
-        buffer(4, half, width),
-        buffer(half, width),
-        buffer(3, 2, half // 2, width),
-        buffer(3, 2, half, width),
+        buffer(4, low, width),
+        buffer(rows - low, width),
+        buffer(3, 2, rows - middle, width),
+        buffer(3, 2, rows - low, width),
     ]
     return pl.pallas_call(
         kernel,
@@ -688,8 +735,10 @@
             jax.ShapeDtypeStruct((16, rows, width), bf16),
         ),
         in_specs=[hbm, vmem, vmem, hbm, hbm, hbm, hbm, hbm, vmem, hbm],
-        out_specs=(hbm, vmem, vmem, vmem, vmem, hbm),
+        out_specs=(hbm,) * 6,
         scratch_shapes=[
+            *[buffer(tok, width)] * 2,
+            *[pltpu.VMEM((rows, width), f32)] * 2,
             buffer(4, tok, width),
             *[buffer(tok, width)] * 4,
             buffer(width // HEAD_DIM, tok, tok),
@@ -701,8 +750,9 @@
             buffer(tok, width),
             buffer(4, 4, tok, 256),
             buffer(chunks, tok, width // chunks),
-            pltpu.VMEM(target.shape, i32),
-            pltpu.VMEM(row.shape, i32),
+            pltpu.VMEM((8, tok), i32),
+            pltpu.VMEM((16, 8, 128), i32),
+            pltpu.VMEM((8, tok), i32),
             pltpu.VMEM((16, 8, 128), i32),
             buffer(chunks, 16, PAD, width // chunks),
             pltpu.VMEM((16, 8, 128), i32),
@@ -716,7 +766,7 @@
             *[dma((2, 8))] * 2,
             *[dma((4, 4))] * 2,
             *[dma((4, 8))] * 2,
-            dma((8,)), dma((2,)), dma((3,)), dma((3,)),
+            dma((8,)), dma((2,)), dma((3,)), dma((3,)), dma((4,)),
         ],
         compiler_params=pltpu.CompilerParams(
             collective_id=0, has_side_effects=True, vmem_limit_bytes=63 * 1024 * 1024
@@ -725,12 +775,49 @@
     )(tile, target, row, wo, vw, query, key, value, position, normed)
 
 
+def copy_kernel(count, *refs):
+    sources, targets, held = refs[:count], refs[count : 2 * count], refs[2 * count : 3 * count]
+    into_sem, out_sem = refs[3 * count :]
+    steps = []
+    for src, dst, buffer in zip(sources, targets, held):
+        rows = src.shape[0] // (8 if src.shape[1] > 1024 else 2)
+        for start in range(0, src.shape[0], rows):
+            span, k = pl.ds(start, rows), len(steps)
+            steps.append(
+                (
+                    pltpu.make_async_copy(src.at[span], buffer.at[span], into_sem.at[k]),
+                    pltpu.make_async_copy(buffer.at[span], dst.at[span], out_sem.at[k]),
+                )
+            )
+    for into, _ in steps:
+        into.start()
+    for into, out in steps:
+        into.wait()
+        out.start()
+    for _, out in steps:
+        out.wait()
+
+
+def copied(arrays):
+    hbm = pl.BlockSpec(memory_space=pl.ANY)
+    return pl.pallas_call(
+        functools.partial(copy_kernel, len(arrays)),
+        out_shape=tuple(jax.ShapeDtypeStruct(array.shape, array.dtype) for array in arrays),
+        in_specs=[hbm] * len(arrays),
+        out_specs=(hbm,) * len(arrays),
+        scratch_shapes=[pltpu.VMEM(array.shape, array.dtype) for array in arrays]
+        + [pltpu.SemaphoreType.DMA((16,))] * 2,
+        compiler_params=pltpu.CompilerParams(vmem_limit_bytes=60 * 1024 * 1024),
+        name="copied",
+    )(*arrays)
+
+
 def shards(boundary_grad, tile_target, tile_row, normed_input, query, keys, values, positions, out_weight, value_weight):
     outputs = backward(
         boundary_grad[0], tile_target, tile_row, out_weight[0], value_weight[0], query[0], keys[0], values[0], positions,
         normed_input[0],
     )
-    return tuple(output[None] for output in outputs[:5])
+    return tuple(output[None] for output in copied(outputs[:5]))
 
 
 def solution(mesh):

time: 185 us -> 178 us (0.962); the launches traced: 181 us -> 178 us
  local copies, waits for them, and re-layouts: 8.74 us -> 0 us
  Pallas kernels: 171 us -> 177 us
    unnamed x13 -> x0, local copies, waits for them, and re-layouts: 8.74 us -> none
    pallas_call x0 -> x1, Pallas kernels: none -> 6.57 us  [copied(): pl.pallas_call(functools.partial(copy_kernel, len(arrays)), out_shape=tup...]
where the time goes in v4:
time: 178 us
  Pallas kernels  177 us (99%)
    pallas_call x1, Pallas kernels, backward(): pl.pallas_call(kernel, out_shape=(jax.ShapeDtypeStruct((tok, 4 * width),...  171 us
    pallas_call x1, Pallas kernels, copied(): pl.pallas_call(functools.partial(copy_kernel, len(arrays)), out_shape=tup...  6.57 us

profile of v4, /device:TPU:27, one launch (start us, length us, event | category | flops | bytes accessed | tf_op | source)
XLA Modules:
  0.0 178.1 jit_solution(13636939378891163466)
XLA Ops:
  0.6 170.7 %relay_backward_and_sum.1 = (bf16[512,4096]{1,0:T(8,128)(2,1)}, bf16[512,1024]{1,0:T(8,128)(2,1)}, bf16[512,1024]{1,0:T(8,128)(2,1)}, f32[256,1024]{1,0:T(8,128)...) custom-call(bf16[512,1024]{1,0:T(8,128)(2,1)} %bitcast.13, s32[1,512]{1,0:T(1,128)} %target_ref.1, ...), custom_call_target="tpu_custom_call" | custom-call | tf_op jit(solution)/shard_map/relay_backward_and_sum/pallas_call | solution.py:727
  171.4 6.6 %copied.1 = (bf16[512,4096]{1,0:T(8,128)(2,1)}, bf16[512,1024]{1,0:T(8,128)(2,1)}, bf16[512,1024]{1,0:T(8,128)(2,1)}, f32[256,1024]{1,0:T(8,128)}, f32[256,1024]{1,0:T(8,128)}) custom-call(bf16[512,4096]{1,0:T(8,128)(2,1)} %get-tuple-element.15.refs_0_, bf16[512,1024]{1,0:T(8,128)(2,1)} %get-tuple-element.16.refs_1_, ...), custom_call_target="tpu_custom_call" | custom-call | tf_op jit(solution)/shard_map/copied/pallas_call | solution.py:803

commit v5 on v4

--- a/solution.py
+++ b/solution.py
@@ -511,31 +511,35 @@
         to_m.wait_recv()
         on_m.start()
 
-    def attend(pair):
+    def gv_pair(pair):
         lanes = pl.ds(pair * 256, 256)
         total = jnp.zeros((tok, 256), jnp.float32)
         for b in range(4):
             block = weight[4 * b : 4 * b + 4, :, lanes].reshape(width, 256)
             total = total + jnp.dot(g_ref[b], block, preferred_element_type=jnp.float32)
         both = total.astype(jnp.bfloat16)
+        gq_ref[:, lanes] = both
+        for h in range(2):
+            gout = both[:, h * HEAD_DIM : (h + 1) * HEAD_DIM]
+            gv = jnp.dot(probs[2 * pair + h], gout, preferred_element_type=jnp.float32).astype(jnp.bfloat16)
+            gv_own[:, pl.ds(pair * 256 + h * HEAD_DIM, HEAD_DIM)] = gv
+            gv_all[at.n, pair, :, pl.ds(h * HEAD_DIM, HEAD_DIM)] = gv
+        to_p, to_m, _, _ = gv_copies(pair)
+        to_p.start()
+        to_m.start()
+
+    def score(pair):
         for h in range(2):
             cols = pl.ds(pair * 256 + h * HEAD_DIM, HEAD_DIM)
-            gout = both[:, h * HEAD_DIM : (h + 1) * HEAD_DIM]
             prob = probs[2 * pair + h]
-            dprob = lax.dot_general(value_ref[:, cols], gout, NT, preferred_element_type=jnp.float32)
+            dprob = lax.dot_general(value_ref[:, cols], gq_ref[:, cols], NT, preferred_element_type=jnp.float32)
             wide_prob = prob.astype(jnp.float32)
             delta = jnp.sum(wide_prob * dprob, axis=0, keepdims=True)
             dscore = (wide_prob * (dprob - delta)).astype(jnp.bfloat16)
-            gv = jnp.dot(prob, gout, preferred_element_type=jnp.float32).astype(jnp.bfloat16)
-            gv_own[:, cols] = gv
-            gv_all[at.n, pair, :, pl.ds(h * HEAD_DIM, HEAD_DIM)] = gv
             gk = jnp.dot(dscore, query_ref[:, cols], preferred_element_type=jnp.float32) * scale
             gk_ref[:, cols] = gk.astype(jnp.bfloat16)
             gq = lax.dot_general(dscore, key_ref[:, cols], TN, preferred_element_type=jnp.float32) * scale
             gq_ref[:, cols] = gq.astype(jnp.bfloat16)
-        to_p, to_m, _, _ = gv_copies(pair)
-        to_p.start()
-        to_m.start()
 
     def load_tile(tile):
         return pltpu.make_async_copy(vw_all.at[pl.ds(4 * tile, 4)], core_out.at[pl.ds(4 * (tile % 2), 4)], tile_sem.at[tile % 2])
@@ -636,23 +640,27 @@
     forward(3)
     theirs_out(2, 6)
     ours_out(0, 6)
-    value_third()
     wait_gathered()
     out_last()
-    attend(0)
+    gv_pair(0)
+    score(0)
+    value_third()
     theirs_out(6, 8)
     ours_out(6, 8)
     out_sum_a()
     out_sum_b()
     drain_core()
     load_normed.start()
-    attend(1)
+    gv_pair(1)
+    score(1)
     forward_gv(0)
     value_fourth()
-    attend(2)
+    gv_pair(2)
+    score(2)
     forward_gv(1)
     out_sum_second()
-    attend(3)
+    gv_pair(3)
+    score(3)
     stores[0].start()
     stores[1].start()
     forward_gv(2)

time: 178 us -> 172 us (0.966)
  Pallas kernels: 177 us -> 171 us
    pallas_call x1, Pallas kernels: 171 us -> 164 us  [backward(): pl.pallas_call(kernel, out_shape=(jax.ShapeDtypeStruct((tok, 4 * width),...]
where the time goes in v5:
time: 172 us; the launch traced here: 171 us
  Pallas kernels  171 us (99%)
    pallas_call x1, Pallas kernels, backward(): pl.pallas_call(kernel, out_shape=(jax.ShapeDtypeStruct((tok, 4 * width),...  164 us
    pallas_call x1, Pallas kernels, copied(): pl.pallas_call(functools.partial(copy_kernel, len(arrays)), out_shape=tup...  6.57 us

profile of v5, /device:TPU:27, one launch (start us, length us, event | category | flops | bytes accessed | tf_op | source)
XLA Modules:
  0.0 171.4 jit_solution(7263896769538287457)
XLA Ops:
  0.6 164.0 %relay_backward_and_sum.1 = (bf16[512,4096]{1,0:T(8,128)(2,1)}, bf16[512,1024]{1,0:T(8,128)(2,1)}, bf16[512,1024]{1,0:T(8,128)(2,1)}, f32[256,1024]{1,0:T(8,128)...) custom-call(bf16[512,1024]{1,0:T(8,128)(2,1)} %bitcast.13, s32[1,512]{1,0:T(1,128)} %target_ref.1, ...), custom_call_target="tpu_custom_call" | custom-call | tf_op jit(solution)/shard_map/relay_backward_and_sum/pallas_call | solution.py:735
  164.6 6.6 %copied.1 = (bf16[512,4096]{1,0:T(8,128)(2,1)}, bf16[512,1024]{1,0:T(8,128)(2,1)}, bf16[512,1024]{1,0:T(8,128)(2,1)}, f32[256,1024]{1,0:T(8,128)}, f32[256,1024]{1,0:T(8,128)}) custom-call(bf16[512,4096]{1,0:T(8,128)(2,1)} %get-tuple-element.15.refs_0_, bf16[512,1024]{1,0:T(8,128)(2,1)} %get-tuple-element.16.refs_1_, ...), custom_call_target="tpu_custom_call" | custom-call | tf_op jit(solution)/shard_map/copied/pallas_call | solution.py:811
